TPU v7x, 256 devices: a whole 4x4x8 slice. The times are simulated.
256 devices in a mesh: gz: 16 (over z, core), gy: 4 (over y), gx: 4 (over x).
Axes of the slice: x: 4, y: 4, z: 8, core: 2. Of those that a mesh axis runs over, the one named last changes fastest.
Arguments:
- forward: float32 [6, 256, 64, 512], P(None, 'gz', 'gy', 'gx'), may hold values from -26 to 26
- adjoint_prev: float32 [6, 256, 64, 512], P(None, 'gz', 'gy', 'gx'), may hold values from -6 to 6
- density: float32 [256, 64, 512], P('gz', 'gy', 'gx'), may hold values from 0.05 to 1
- labels: int32 [256, 64, 512], P('gz', 'gy', 'gx'), may hold values from 0 to 2
- ports: int32 [256, 64, 512], P('gz', 'gy', 'gx'), may hold values 0 or 1
- z_target: float32 [2], replicated, may hold values from -4 to 4
- radius_z: int32 [256], replicated, may hold values from 8 to 16, as said below
- radius_y: int32 [64], replicated, may hold values from 8 to 16, as said below
- radius_x: int32 [512], replicated, may hold values from 8 to 16, as said below
Outputs:
- adjoint: float32 [6, 256, 64, 512], P(None, 'gz', 'gy', 'gx')
- gradient: float32 [256, 64, 512], P('gz', 'gy', 'gx')
- impedance: float32 [2], replicated
Inputs may be any that keep to these rules, and one draw needn't show every extreme that they name: `labels`: 0 air, 1 coil, 2 design. `ports`: 1 marks a port cell. `radius_z`: both ends of the range occur along the axis. `radius_y`: both ends of the range occur along the axis. `radius_x`: both ends of the range occur along the axis.
All inputs are finite; a program needn't handle non-finite values. No bound on the sum of `ports` on one device may be relied on, other than what follows from the above.
Results may differ from a plain program's by a relative error of at most 0.0001.
Values sent between devices are 32-bit elements; how exact they have to be, the bound alone decides.
A program may use at most 64 MiB of HBM per device.

v0:
```python
import jax
import jax.numpy as jnp
from jax import lax
from jax.sharding import PartitionSpec as P

SWEEPS = 2
RADIUS = 16


MU_GAIN = 19.0
KAPPA_GAIN = 2.0
RELAX = 0.8
SENS_GAIN = 0.1


def with_halo(block, sides, width):
    for axis, dim in sides:
        count = lax.axis_size(axis)
        forward = [(i, i + 1) for i in range(count - 1)]
        backward = [(target, source) for source, target in forward]
        low = lax.ppermute(
            lax.slice_in_dim(block, block.shape[dim] - width, None, axis=dim), axis, forward
        )
        high = lax.ppermute(lax.slice_in_dim(block, 0, width, axis=dim), axis, backward)
        block = jnp.concatenate([low, block, high], axis=dim)
    return block


def material(labels, density):
    design = (labels == 2).astype(jnp.float32)
    square = density * density
    density_cube = square * density
    nu_design = 1.0 / (1.0 + MU_GAIN * density_cube)
    nu_cell = 1.0 - design + design * nu_design
    kappa_sigma = design * KAPPA_GAIN * density_cube
    nu_slope = -3.0 * MU_GAIN * design * square * nu_design * nu_design
    sigma_slope = 3.0 * KAPPA_GAIN * design * square
    return (nu_cell, kappa_sigma, nu_slope, sigma_slope)


def neighbours(padded):
    return [
        padded[..., 2:, 1:-1, 1:-1],
        padded[..., :-2, 1:-1, 1:-1],
        padded[..., 1:-1, 2:, 1:-1],
        padded[..., 1:-1, :-2, 1:-1],
        padded[..., 1:-1, 1:-1, 2:],
        padded[..., 1:-1, 1:-1, :-2],
    ]


def relax_step(current, padded, face_nu, diag_re, kappa_sigma, source):
    applied = diag_re * current
    for nu_face, beside in zip(face_nu, neighbours(padded)):
        applied = applied - nu_face * beside
    image_re = applied[:3] - kappa_sigma * current[3:]
    image_im = applied[3:] + kappa_sigma * current[:3]
    rest_re = source[:3] - image_re
    rest_im = source[3:] - image_im
    denominator = diag_re * diag_re + kappa_sigma * kappa_sigma
    step_re = (rest_re * diag_re + rest_im * kappa_sigma) / denominator
    step_im = (rest_im * diag_re - rest_re * kappa_sigma) / denominator
    return current + RELAX * jnp.concatenate([step_re, step_im], axis=0)


def sensitivity(adjoint, padded_adj, forward, padded_fwd, nu_slope, sigma_slope):
    energy = jnp.zeros(forward.shape[1:], jnp.float32)
    for adj_near, fwd_near in zip(neighbours(padded_adj), neighbours(padded_fwd)):
        diff_adj = adjoint - adj_near
        diff_fwd = forward - fwd_near
        energy = energy + jnp.sum(diff_adj[:3] * diff_fwd[:3] - diff_adj[3:] * diff_fwd[3:], axis=0)
    cross_term = jnp.sum(adjoint[:3] * forward[3:] + adjoint[3:] * forward[:3], axis=0)
    power_term = jnp.sum(forward * forward, axis=0)
    return SENS_GAIN * (-nu_slope * 0.5 * energy + sigma_slope * (cross_term + power_term))


def band_matrix(radius_rows, count, shift):
    row_count = radius_rows.shape[0]
    source_pos = lax.broadcasted_iota(jnp.int32, (row_count, count), 0)
    target_pos = lax.broadcasted_iota(jnp.int32, (row_count, count), 1)
    distance = jnp.abs(source_pos - shift - target_pos)
    return jnp.maximum(radius_rows[:, None] + 1 - distance, 0).astype(jnp.float32)


def port_pattern(port_mask, coef_re, coef_im):
    zeros_plane = jnp.zeros_like(port_mask)
    return jnp.stack(
        [
            zeros_plane,
            zeros_plane,
            coef_re * port_mask,
            zeros_plane,
            zeros_plane,
            coef_im * port_mask,
        ],
        axis=0,
    )


def local_rows(radius, offset, count):
    whole_count = radius.shape[0]
    own_radius = lax.dynamic_slice_in_dim(radius, offset, count)
    norm_rows = jnp.sum(band_matrix(own_radius, whole_count, -offset), axis=1)
    padded = jnp.pad(radius, (RADIUS, RADIUS))
    beside_all = lax.dynamic_slice_in_dim(padded, offset, count + 2 * RADIUS)
    return (norm_rows, band_matrix(beside_all, count, RADIUS))


def extend(current):
    return with_halo(current, (("gz", 1), ("gy", 2), ("gx", 3)), 1)


def body(forward, adjoint_prev, density, labels, ports, z_target, radius_z, radius_y, radius_x):
    depth_cells, height_cells, width_cells = density.shape
    total_z = depth_cells * lax.axis_size("gz")
    total_y = height_cells * lax.axis_size("gy")
    total_x = width_cells * lax.axis_size("gx")
    nu_cell, kappa_sigma, nu_slope, sigma_slope = material(labels, density)
    port_mask = ports.astype(jnp.float32)
    joined = jnp.concatenate([forward, nu_cell[None] - 1.0], axis=0)
    padded_all = with_halo(joined, (("gz", 1), ("gy", 2), ("gx", 3)), 1)
    padded_fwd = padded_all[:6]
    face_nu = [0.5 * (nu_cell + (1.0 + beside)) for beside in neighbours(padded_all[6])]
    diag_re = face_nu[0]
    for nu_face in face_nu[1:]:
        diag_re = diag_re + nu_face
    port_re = jnp.sum(port_mask * forward[2])
    port_im = jnp.sum(port_mask * forward[5])
    link_scale = 4.0 / (total_z * total_y * total_x)
    joule_source = kappa_sigma * forward
    padded_adj = None
    totals = lax.psum((port_re, port_im), ("gz", "gy", "gx"))
    link_re = link_scale * totals[0]
    link_im = link_scale * totals[1]
    coef_re = 2.0 * (link_re - z_target[0])
    coef_im = -2.0 * (link_im - z_target[1])
    source = joule_source + port_pattern(port_mask, coef_re, coef_im)
    adjoint = adjoint_prev
    for sweep_index in range(SWEEPS):
        adjoint = relax_step(adjoint, extend(adjoint), face_nu, diag_re, kappa_sigma, source)
    padded_adj = extend(adjoint)
    sens_field = sensitivity(adjoint, padded_adj, forward, padded_fwd, nu_slope, sigma_slope)
    norm_z, band_z = local_rows(radius_z, lax.axis_index("gz") * depth_cells, depth_cells)
    norm_y, band_y = local_rows(radius_y, lax.axis_index("gy") * height_cells, height_cells)
    norm_x, band_x = local_rows(radius_x, lax.axis_index("gx") * width_cells, width_cells)
    scaled = sens_field / (norm_z[:, None, None] * norm_y[None, :, None] * norm_x[None, None, :])
    highest = lax.Precision.HIGHEST
    plane_ext = with_halo(scaled, (("gy", 1), ("gx", 2)), RADIUS)
    along_x = jnp.einsum("zya,aj->zyj", plane_ext, band_x, precision=highest)
    along_y = jnp.einsum("zbx,bk->zkx", along_x, band_y, precision=highest)
    deep_ext = with_halo(along_y, (("gz", 0),), RADIUS)
    filtered = jnp.einsum("ayx,aj->jyx", deep_ext, band_z, precision=highest)
    return (adjoint, filtered, jnp.stack([link_re, link_im]))


def solution(mesh):
    in_specs = (
        P(None, "gz", "gy", "gx"),
        P(None, "gz", "gy", "gx"),
        P("gz", "gy", "gx"),
        P("gz", "gy", "gx"),
        P("gz", "gy", "gx"),
        P(),
        P(),
        P(),
        P(),
    )
    out_specs = (P(None, "gz", "gy", "gx"), P("gz", "gy", "gx"), P())
    return jax.shard_map(body, mesh=mesh, in_specs=in_specs, out_specs=out_specs, check_vma=False)
```

profile of v0, /device:TPU:1, one launch (start us, length us, event | category | flops | bytes accessed | tf_op | source)
XLA Modules:
  0.0 264.9 jit_solution(14098634830209528091)
XLA Ops:
  1.6 5.1 %collective-permute-start.6 = (f32[6,1,16,128]{3,2,1,0:T(8,128)S(1)}, f32[6,1,16,128]{3,2,1,0:T(8,128)S(1)}, u32[]{:S(2)}, u32[]{:S(2)}) collective-permute-start(f32[6,1,16,128]{3,2,1,0:T(8,128)S(1)} %get-tuple-element.70), channel_id=1, source_target_pairs={{16,0},{32,16},{48,32},{64,48},{80,64},{96,80},{112,96},{128,112},... | collective-permute-start | bytes 147464 | tf_op jit(solution)/shard_map/ppermute | solution.py:24
  6.8 1.9 collective-permute-start.7
  10.6 2.2 collective-permute-start
  12.8 2.1 collective-permute-start.1
  15.6 1.5 fusion.98
  17.2 79.5 %all-reduce.3 = (f32[]{:T(128)}, f32[]{:T(128)}) all-reduce(f32[]{:T(128)} %get-tuple-element.16, f32[]{:T(128)} %get-tuple-element.15), channel_id=1, replica_groups=mesh['gz'=16,'gy'=4,'gx'=4] {'gz','gy','gx'}, use_global_device_ids=true, to_apply=%region_3.0 | all-reduce | flops 2 | bytes 16 | tf_op jit(solution)/shard_map/psum | solution.py:132
  103.4 4.0 %collective-permute-start.2 = (f32[7,18,1,128]{3,2,1,0:T(1,128)S(1)}, f32[7,18,1,128]{3,2,1,0:T(1,128)S(1)}, u32[]{:S(2)}, u32[]{:S(2)}) collective-permute-start(f32[7,18,1,128]{3,2,1,0:T(1,128)S(1)} %get-tuple-element.46), channel_id=1, source_target_pairs={{0,4},{4,8},{8,12},{1,5},{5,9},{9,13},{2,6},{6,10},{10,14},{3,7},{... | collective-permute-start | bytes 193544 | tf_op jit(solution)/shard_map/ppermute | solution.py:21
  110.2 1.5 fusion.138
  111.7 2.9 %copy.129 = f32[6,18,18,1]{2,1,3,0:T(8,128)} copy(f32[6,18,18,1]{3,2,1,0:T(8,128)} %get-tuple-element.40) | data formatting | bytes 15552
  114.5 1.6 copy.130
  116.1 2.7 %collective-permute-start.11 = (f32[6,18,18,1]{2,1,3,0:T(8,128)}, f32[6,18,18,1]{2,1,3,0:T(8,128)}, u32[]{:S(2)}, u32[]{:S(2)}) collective-permute-start(f32[6,18,18,1]{2,1,3,0:T(8,128)} %copy.130), channel_id=1, source_target_pairs={{0,1},{1,2},{2,3},{4,5},{5,6},{6,7},{8,9},{9,10},{10,11},{12,13},{... | collective-permute-start | bytes 23336 | tf_op jit(solution)/shard_map/ppermute | solution.py:21
  120.4 1.7 fusion.135
  122.1 2.8 %copy.109 = f32[7,18,18,1]{2,3,1,0:T(1,128)} copy(f32[7,18,18,1]{3,2,1,0:T(8,128)} %get-tuple-element.34) | data formatting | bytes 18144 | tf_op jit(solution)/shard_map/slice | solution.py:22
  127.7 5.2 %collective-permute-start.4 = (f32[7,18,18,1]{2,3,1,0:T(1,128)}, f32[7,18,18,1]{2,3,1,0:T(1,128)}, u32[]{:S(2)}, u32[]{:S(2)}) collective-permute-start(f32[7,18,18,1]{2,3,1,0:T(1,128)} %copy.109), channel_id=1, source_target_pairs={{0,1},{1,2},{2,3},{4,5},{5,6},{6,7},{8,9},{9,10},{10,11},{12,13},{... | collective-permute-start | bytes 27224 | tf_op jit(solution)/shard_map/ppermute | solution.py:21
  133.6 2.7 %copy.114 = f32[6,18,18,1]{3,2,1,0:T(8,128)} copy(f32[6,18,18,1]{2,1,3,0:T(8,128)} %collective-permute-done.10) | data formatting | bytes 15552 | tf_op jit(solution)/shard_map/ppermute | solution.py:24
  136.3 2.7 %copy.116 = f32[6,18,18,1]{3,2,1,0:T(8,128)} copy(f32[6,18,18,1]{2,1,3,0:T(8,128)} %collective-permute-done.11) | data formatting | bytes 15552 | tf_op jit(solution)/shard_map/ppermute | solution.py:21
  139.1 1.7 copy.111
  140.8 2.9 %copy.112 = f32[7,18,18,1]{3,2,1,0:T(8,128)} copy(f32[7,18,18,1]{2,3,1,0:T(1,128)} %collective-permute-done.5) | data formatting | bytes 18144 | tf_op jit(solution)/shard_map/ppermute | solution.py:24
  146.1 2.2 fusion.6
  150.4 5.5 %collective-permute-start.13 = (f32[6,1,16,128]{3,2,1,0:T(8,128)S(1)}, f32[6,1,16,128]{3,2,1,0:T(8,128)S(1)}, u32[]{:S(2)}, u32[]{:S(2)}) collective-permute-start(f32[6,1,16,128]{3,2,1,0:T(8,128)S(1)} %get-tuple-element.68), channel_id=1, source_target_pairs={{0,16},{16,32},{32,48},{48,64},{64,80},{80,96},{96,112},{112,128},... | collective-permute-start | bytes 147464 | tf_op jit(solution)/shard_map/ppermute | solution.py:21
  155.9 1.9 collective-permute-start.12
  157.9 3.4 %collective-permute-done.12 = f32[6,1,16,128]{3,2,1,0:T(8,128)S(1)} collective-permute-done((f32[6,1,16,128]{3,2,1,0:T(8,128)S(1)}, f32[6,1,16,128]{3,2,1,0:T(8,128)S(1)}, u32[]{:S(2)}, u32[]{:S(2)}) %collective-permute-start.12) | collective-permute-done | bytes 49184 | tf_op jit(solution)/shard_map/ppermute | solution.py:24
  161.4 4.3 %collective-permute-start.15 = (f32[6,18,1,128]{3,2,1,0:T(1,128)S(1)}, f32[6,18,1,128]{3,2,1,0:T(1,128)S(1)}, u32[]{:S(2)}, u32[]{:S(2)}) collective-permute-start(f32[6,18,1,128]{3,2,1,0:T(1,128)S(1)} %get-tuple-element.57), channel_id=1, source_target_pairs={{0,4},{4,8},{8,12},{1,5},{5,9},{9,13},{2,6},{6,10},{10,14},{3,7},{... | collective-permute-start | bytes 165896 | tf_op jit(solution)/shard_map/ppermute | solution.py:21
  167.1 3.5 %collective-permute-done.14 = f32[6,18,1,128]{3,2,1,0:T(1,128)S(1)} collective-permute-done((f32[6,18,1,128]{3,2,1,0:T(1,128)S(1)}, f32[6,18,1,128]{3,2,1,0:T(1,128)S(1)}, u32[]{:S(2)}, u32[]{:S(2)}) %collective-permute-start.14) | collective-permute-done | bytes 55328 | tf_op jit(solution)/shard_map/ppermute | solution.py:24
  170.8 2.0 fusion.137
  172.7 2.3 copy.131
  175.0 2.3 copy.132
  177.3 3.0 %collective-permute-start.17 = (f32[6,18,18,1]{2,1,3,0:T(8,128)S(1)}, f32[6,18,18,1]{2,1,3,0:T(8,128)S(1)}, u32[]{:S(2)}, u32[]{:S(2)}) collective-permute-start(f32[6,18,18,1]{2,1,3,0:T(8,128)S(1)} %copy.132), channel_id=1, source_target_pairs={{0,1},{1,2},{2,3},{4,5},{5,6},{6,7},{8,9},{9,10},{10,11},{12,13},{... | collective-permute-start | bytes 23336 | tf_op jit(solution)/shard_map/ppermute | solution.py:21
  182.0 4.3 %collective-permute-done.16 = f32[6,18,18,1]{2,1,3,0:T(8,128)S(1)} collective-permute-done((f32[6,18,18,1]{2,1,3,0:T(8,128)S(1)}, f32[6,18,18,1]{2,1,3,0:T(8,128)S(1)}, u32[]{:S(2)}, u32[]{:S(2)}) %collective-permute-start.16) | collective-permute-done | bytes 7808 | tf_op jit(solution)/shard_map/ppermute | solution.py:24
  186.3 1.9 copy.118
  188.1 1.8 copy.120
  190.0 2.9 %fusion.13 = f32[6,16,16,128]{3,2,1,0:T(8,128)S(1)} fusion(f32[6,18,18,1]{3,2,1,0:T(8,128)} %copy.120, f32[6,18,1,128]{3,2,1,0:T(1,128)} %copy-done.35, f32[6,18,1,128]{3,2,1,0:T(1,128)} %copy-done.34, f32[6,1,16,128]{3,2,1,0:T(8,128)S(1)} %collective-permute-done.12, f32[6,16,16,128]{3,2,1,0:T(8,128)S(1)} %fusion.36, ...), kind=kLoop, calls=%fused_computation.63 | loop fusion | flops 6094848 | bytes 2714816 | tf_op jit(solution)/shard_map/sub | solution.py:55
  193.3 4.1 %collective-permute-start.19 = (f32[6,1,16,128]{3,2,1,0:T(8,128)S(1)}, f32[6,1,16,128]{3,2,1,0:T(8,128)S(1)}, u32[]{:S(2)}, u32[]{:S(2)}) collective-permute-start(f32[6,1,16,128]{3,2,1,0:T(8,128)S(1)} %get-tuple-element.66), channel_id=1, source_target_pairs={{0,16},{16,32},{32,48},{48,64},{64,80},{80,96},{96,112},{112,128},... | collective-permute-start | bytes 147464 | tf_op jit(solution)/shard_map/ppermute | solution.py:21
  197.4 1.9 collective-permute-start.18
  199.4 2.3 fusion.2
  202.9 2.7 %collective-permute-start.21 = (f32[6,18,1,128]{3,2,1,0:T(1,128)S(1)}, f32[6,18,1,128]{3,2,1,0:T(1,128)S(1)}, u32[]{:S(2)}, u32[]{:S(2)}) collective-permute-start(f32[6,18,1,128]{3,2,1,0:T(1,128)S(1)} %get-tuple-element.55), channel_id=1, source_target_pairs={{0,4},{4,8},{8,12},{1,5},{5,9},{9,13},{2,6},{6,10},{10,14},{3,7},{... | collective-permute-start | bytes 165896 | tf_op jit(solution)/shard_map/ppermute | solution.py:21
  207.1 3.8 %collective-permute-done.20 = f32[6,18,1,128]{3,2,1,0:T(1,128)S(1)} collective-permute-done((f32[6,18,1,128]{3,2,1,0:T(1,128)S(1)}, f32[6,18,1,128]{3,2,1,0:T(1,128)S(1)}, u32[]{:S(2)}, u32[]{:S(2)}) %collective-permute-start.20) | collective-permute-done | bytes 55328 | tf_op jit(solution)/shard_map/ppermute | solution.py:24
  212.5 2.3 copy.133
  215.7 2.2 collective-permute-start.23
  220.3 3.7 %collective-permute-done.22 = f32[6,18,18,1]{2,1,3,0:T(8,128)} collective-permute-done((f32[6,18,18,1]{2,1,3,0:T(8,128)S(1)}, f32[6,18,18,1]{2,1,3,0:T(8,128)}, u32[]{:S(2)}, u32[]{:S(2)}) %collective-permute-start.22) | collective-permute-done | bytes 7808 | tf_op jit(solution)/shard_map/ppermute | solution.py:24
  224.0 1.7 copy.122
  225.7 1.8 copy.125
  227.5 2.3 fusion.3
  235.2 4.0 %collective-permute-start.24 = (f32[16,16,128]{2,1,0:T(8,128)S(1)}, f32[16,16,128]{2,1,0:T(8,128)S(1)}, u32[]{:S(2)}, u32[]{:S(2)}) collective-permute-start(f32[16,16,128]{2,1,0:T(8,128)S(1)} %fusion.81), channel_id=1, source_target_pairs={{0,4},{4,8},{8,12},{1,5},{5,9},{9,13},{2,6},{6,10},{10,14},{3,7},{... | collective-permute-start | bytes 393224 | tf_op jit(solution)/shard_map/ppermute | solution.py:21
  244.4 5.4 %collective-permute-done.26 = f32[16,48,16]{2,1,0:T(8,128)S(1)} collective-permute-done((f32[16,48,16]{2,1,0:T(8,128)S(1)}, f32[16,48,16]{2,1,0:T(8,128)S(1)}, u32[]{:S(2)}, u32[]{:S(2)}) %collective-permute-start.26) | collective-permute-done | bytes 49184 | tf_op jit(solution)/shard_map/ppermute | solution.py:21
  249.9 3.9 %collective-permute-done.27 = f32[16,48,16]{2,1,0:T(8,128)S(1)} collective-permute-done((f32[16,48,16]{2,1,0:T(8,128)S(1)}, f32[16,48,16]{2,1,0:T(8,128)S(1)}, u32[]{:S(2)}, u32[]{:S(2)}) %collective-permute-start.27) | collective-permute-done | bytes 49184 | tf_op jit(solution)/shard_map/ppermute | solution.py:24
  255.0 4.7 %collective-permute-start.29 = (f32[16,16,128]{2,1,0:T(8,128)S(1)}, f32[16,16,128]{2,1,0:T(8,128)S(1)}, u32[]{:S(2)}, u32[]{:S(2)}) collective-permute-start(f32[16,16,128]{2,1,0:T(8,128)S(1)} %convolution_bitcast_fusion), channel_id=1, source_target_pairs={{16,0},{32,16},{48,32},{64,48},{80,64},{96,80},{112,96},{128,112},... | collective-permute-start | bytes 393224 | tf_op jit(solution)/shard_map/ppermute | solution.py:24
  259.7 2.1 collective-permute-start.28
  (187 shorter events, 45.9 us)
Async XLA Ops:
  0.6 99.8 %copy-start.5 = (f32[6,16,16,128]{3,2,1,0:T(8,128)S(1)}, f32[6,16,16,128]{3,2,1,0:T(8,128)}, u32[]{:S(2)}) copy-start(f32[6,16,16,128]{3,2,1,0:T(8,128)} %param.10) | copy-start | bytes 2359300
  0.6 15.0 %copy-start = (f32[6,16,16,128]{3,2,1,0:T(8,128)S(1)}, f32[6,16,16,128]{3,2,1,0:T(8,128)}, u32[]{:S(2)}) copy-start(f32[6,16,16,128]{3,2,1,0:T(8,128)} %param.9) | copy-start | bytes 2359300
  0.7 14.3 %copy-start.46 = (f32[2]{0:T(128)S(1)}, f32[2]{0:T(128)}, u32[]{:S(2)}) copy-start(f32[2]{0:T(128)} %param.14) | copy-start | bytes 28
  0.7 98.9 %copy-start.30 = (s32[16,16,128]{2,1,0:T(8,128)S(1)}, s32[16,16,128]{2,1,0:T(8,128)}, u32[]{:S(2)}) copy-start(s32[16,16,128]{2,1,0:T(8,128)} %param.13) | copy-start | bytes 393220
  0.7 97.3 %copy-start.45 = (s32[256]{0:T(256)S(1)}, s32[256]{0:T(256)}, u32[]{:S(2)}) copy-start(s32[256]{0:T(256)} %param.15) | copy-start | bytes 3076
  0.7 99.6 %copy-start.47 = (s32[64]{0:T(128)S(1)}, s32[64]{0:T(128)}, u32[]{:S(2)}) copy-start(s32[64]{0:T(128)} %param.16) | copy-start | bytes 772
  1.6 98.8 %collective-permute-start.6 = (f32[6,1,16,128]{3,2,1,0:T(8,128)S(1)}, f32[6,1,16,128]{3,2,1,0:T(8,128)S(1)}, u32[]{:S(2)}, u32[]{:S(2)}) collective-permute-start(f32[6,1,16,128]{3,2,1,0:T(8,128)S(1)} %get-tuple-element.70), channel_id=1, source_target_pairs={{16,0},{32,16},{48,32},{64,48},{80,64},{96,80},{112,96},{128,112},... | collective-permute-start | bytes 147464 | tf_op jit(solution)/shard_map/ppermute | solution.py:24
  6.8 93.6 %collective-permute-start.7 = (f32[6,1,16,128]{3,2,1,0:T(8,128)S(1)}, f32[6,1,16,128]{3,2,1,0:T(8,128)S(1)}, u32[]{:S(2)}, u32[]{:S(2)}) collective-permute-start(f32[6,1,16,128]{3,2,1,0:T(8,128)S(1)} %get-tuple-element.71), channel_id=1, source_target_pairs={{0,16},{16,32},{32,48},{48,64},{64,80},{80,96},{96,112},{112,128},... | collective-permute-start | bytes 147464 | tf_op jit(solution)/shard_map/ppermute | solution.py:21
  10.6 92.7 %collective-permute-start = (f32[7,1,16,128]{3,2,1,0:T(8,128)S(1)}, f32[7,1,16,128]{3,2,1,0:T(8,128)S(1)}, u32[]{:S(2)}, u32[]{:S(2)}) collective-permute-start(f32[7,1,16,128]{3,2,1,0:T(8,128)S(1)} %get-tuple-element.53), channel_id=1, source_target_pairs={{0,16},{16,32},{32,48},{48,64},{64,80},{80,96},{96,112},{112,128},... | collective-permute-start | bytes 172040 | tf_op jit(solution)/shard_map/ppermute | solution.py:21
  12.8 90.5 %collective-permute-start.1 = (f32[7,1,16,128]{3,2,1,0:T(8,128)S(1)}, f32[7,1,16,128]{3,2,1,0:T(8,128)S(1)}, u32[]{:S(2)}, u32[]{:S(2)}) collective-permute-start(f32[7,1,16,128]{3,2,1,0:T(8,128)S(1)} %get-tuple-element.54), channel_id=1, source_target_pairs={{16,0},{32,16},{48,32},{64,48},{80,64},{96,80},{112,96},{128,112},... | collective-permute-start | bytes 172040 | tf_op jit(solution)/shard_map/ppermute | solution.py:24
  100.5 8.2 %copy-start.10 = (f32[6,18,16,128]{3,2,1,0:T(8,128)}, f32[6,18,16,128]{3,2,1,0:T(8,128)S(1)}, u32[]{:S(2)}) copy-start(f32[6,18,16,128]{3,2,1,0:T(8,128)S(1)} %constant_dynamic-update-slice_fusion) | copy-start | bytes 2654212
  100.6 8.1 %collective-permute-start.9 = (f32[6,18,1,128]{3,2,1,0:T(1,128)S(1)}, f32[6,18,1,128]{3,2,1,0:T(1,128)S(1)}, u32[]{:S(2)}, u32[]{:S(2)}) collective-permute-start(f32[6,18,1,128]{3,2,1,0:T(1,128)S(1)} %get-tuple-element.59), channel_id=1, source_target_pairs={{0,4},{4,8},{8,12},{1,5},{5,9},{9,13},{2,6},{6,10},{10,14},{3,7},{... | collective-permute-start | bytes 165896 | tf_op jit(solution)/shard_map/ppermute | solution.py:21
  102.0 6.8 %collective-permute-start.8 = (f32[6,18,1,128]{3,2,1,0:T(1,128)S(1)}, f32[6,18,1,128]{3,2,1,0:T(1,128)S(1)}, u32[]{:S(2)}, u32[]{:S(2)}) collective-permute-start(f32[6,18,1,128]{3,2,1,0:T(1,128)S(1)} %get-tuple-element.60), channel_id=1, source_target_pairs={{4,0},{8,4},{12,8},{5,1},{9,5},{13,9},{6,2},{10,6},{14,10},{7,3},{... | collective-permute-start | bytes 165896 | tf_op jit(solution)/shard_map/ppermute | solution.py:24
  103.4 16.7 %collective-permute-start.2 = (f32[7,18,1,128]{3,2,1,0:T(1,128)S(1)}, f32[7,18,1,128]{3,2,1,0:T(1,128)S(1)}, u32[]{:S(2)}, u32[]{:S(2)}) collective-permute-start(f32[7,18,1,128]{3,2,1,0:T(1,128)S(1)} %get-tuple-element.46), channel_id=1, source_target_pairs={{0,4},{4,8},{8,12},{1,5},{5,9},{9,13},{2,6},{6,10},{10,14},{3,7},{... | collective-permute-start | bytes 193544 | tf_op jit(solution)/shard_map/ppermute | solution.py:21
  107.4 12.7 %collective-permute-start.3 = (f32[7,18,1,128]{3,2,1,0:T(1,128)S(1)}, f32[7,18,1,128]{3,2,1,0:T(1,128)S(1)}, u32[]{:S(2)}, u32[]{:S(2)}) collective-permute-start(f32[7,18,1,128]{3,2,1,0:T(1,128)S(1)} %get-tuple-element.47), channel_id=1, source_target_pairs={{4,0},{8,4},{12,8},{5,1},{9,5},{13,9},{6,2},{10,6},{14,10},{7,3},{... | collective-permute-start | bytes 193544 | tf_op jit(solution)/shard_map/ppermute | solution.py:24
  116.1 20.2 %collective-permute-start.11 = (f32[6,18,18,1]{2,1,3,0:T(8,128)}, f32[6,18,18,1]{2,1,3,0:T(8,128)}, u32[]{:S(2)}, u32[]{:S(2)}) collective-permute-start(f32[6,18,18,1]{2,1,3,0:T(8,128)} %copy.130), channel_id=1, source_target_pairs={{0,1},{1,2},{2,3},{4,5},{5,6},{6,7},{8,9},{9,10},{10,11},{12,13},{... | collective-permute-start | bytes 23336 | tf_op jit(solution)/shard_map/ppermute | solution.py:21
  118.8 14.8 %collective-permute-start.10 = (f32[6,18,18,1]{2,1,3,0:T(8,128)}, f32[6,18,18,1]{2,1,3,0:T(8,128)}, u32[]{:S(2)}, u32[]{:S(2)}) collective-permute-start(f32[6,18,18,1]{2,1,3,0:T(8,128)} %copy.129), channel_id=1, source_target_pairs={{1,0},{2,1},{3,2},{5,4},{6,5},{7,6},{9,8},{10,9},{11,10},{13,12},{... | collective-permute-start | bytes 23336 | tf_op jit(solution)/shard_map/ppermute | solution.py:24
  120.1 23.5 %copy-start.24 = (f32[7,18,1,128]{3,2,1,0:T(1,128)}, f32[7,18,1,128]{3,2,1,0:T(1,128)S(1)}, u32[]{:S(2)}) copy-start(f32[7,18,1,128]{3,2,1,0:T(1,128)S(1)} %collective-permute-done.2) | copy-start | bytes 193540
  120.2 23.5 %copy-start.27 = (f32[7,18,1,128]{3,2,1,0:T(1,128)}, f32[7,18,1,128]{3,2,1,0:T(1,128)S(1)}, u32[]{:S(2)}) copy-start(f32[7,18,1,128]{3,2,1,0:T(1,128)S(1)} %collective-permute-done.3) | copy-start | bytes 193540
  126.4 14.4 %collective-permute-start.5 = (f32[7,18,18,1]{2,3,1,0:T(1,128)}, f32[7,18,18,1]{2,3,1,0:T(1,128)}, u32[]{:S(2)}, u32[]{:S(2)}) collective-permute-start(f32[7,18,18,1]{2,3,1,0:T(1,128)} %copy.110), channel_id=1, source_target_pairs={{1,0},{2,1},{3,2},{5,4},{6,5},{7,6},{9,8},{10,9},{11,10},{13,12},{... | collective-permute-start | bytes 27224 | tf_op jit(solution)/shard_map/ppermute | solution.py:24
  127.7 11.4 %collective-permute-start.4 = (f32[7,18,18,1]{2,3,1,0:T(1,128)}, f32[7,18,18,1]{2,3,1,0:T(1,128)}, u32[]{:S(2)}, u32[]{:S(2)}) collective-permute-start(f32[7,18,18,1]{2,3,1,0:T(1,128)} %copy.109), channel_id=1, source_target_pairs={{0,1},{1,2},{2,3},{4,5},{5,6},{6,7},{8,9},{9,10},{10,11},{12,13},{... | collective-permute-start | bytes 27224 | tf_op jit(solution)/shard_map/ppermute | solution.py:21
  140.8 4.2 %copy-start.2 = (f32[7,18,18,1]{3,2,1,0:T(8,128)}, f32[7,18,18,1]{3,2,1,0:T(8,128)S(1)}, u32[]{:S(2)}) copy-start(f32[7,18,18,1]{3,2,1,0:T(8,128)S(1)} %copy.111) | copy-start | bytes 27220
  150.2 7.6 %copy-start.48 = (f32[16]{0:T(128)S(1)}, f32[16]{0:T(128)}, u32[]{:S(2)}) copy-start(f32[16]{0:T(128)} %convert_reduce_fusion.2) | copy-start | bytes 196
  150.2 16.8 %copy-start.44 = (s32[512]{0:T(512)S(1)}, s32[512]{0:T(512)}, u32[]{:S(2)}) copy-start(s32[512]{0:T(512)} %param.17) | copy-start | bytes 6148
  150.4 7.6 %collective-permute-start.13 = (f32[6,1,16,128]{3,2,1,0:T(8,128)S(1)}, f32[6,1,16,128]{3,2,1,0:T(8,128)S(1)}, u32[]{:S(2)}, u32[]{:S(2)}) collective-permute-start(f32[6,1,16,128]{3,2,1,0:T(8,128)S(1)} %get-tuple-element.68), channel_id=1, source_target_pairs={{0,16},{16,32},{32,48},{48,64},{64,80},{80,96},{96,112},{112,128},... | collective-permute-start | bytes 147464 | tf_op jit(solution)/shard_map/ppermute | solution.py:21
  155.9 5.4 %collective-permute-start.12 = (f32[6,1,16,128]{3,2,1,0:T(8,128)S(1)}, f32[6,1,16,128]{3,2,1,0:T(8,128)S(1)}, u32[]{:S(2)}, u32[]{:S(2)}) collective-permute-start(f32[6,1,16,128]{3,2,1,0:T(8,128)S(1)} %get-tuple-element.69), channel_id=1, source_target_pairs={{16,0},{32,16},{48,32},{64,48},{80,64},{96,80},{112,96},{128,112},... | collective-permute-start | bytes 147464 | tf_op jit(solution)/shard_map/ppermute | solution.py:24
  161.4 5.7 %collective-permute-start.15 = (f32[6,18,1,128]{3,2,1,0:T(1,128)S(1)}, f32[6,18,1,128]{3,2,1,0:T(1,128)S(1)}, u32[]{:S(2)}, u32[]{:S(2)}) collective-permute-start(f32[6,18,1,128]{3,2,1,0:T(1,128)S(1)} %get-tuple-element.57), channel_id=1, source_target_pairs={{0,4},{4,8},{8,12},{1,5},{5,9},{9,13},{2,6},{6,10},{10,14},{3,7},{... | collective-permute-start | bytes 165896 | tf_op jit(solution)/shard_map/ppermute | solution.py:21
  165.7 4.9 %collective-permute-start.14 = (f32[6,18,1,128]{3,2,1,0:T(1,128)S(1)}, f32[6,18,1,128]{3,2,1,0:T(1,128)S(1)}, u32[]{:S(2)}, u32[]{:S(2)}) collective-permute-start(f32[6,18,1,128]{3,2,1,0:T(1,128)S(1)} %get-tuple-element.58), channel_id=1, source_target_pairs={{4,0},{8,4},{12,8},{5,1},{9,5},{13,9},{6,2},{10,6},{14,10},{7,3},{... | collective-permute-start | bytes 165896 | tf_op jit(solution)/shard_map/ppermute | solution.py:24
  167.1 5.7 %copy-start.34 = (f32[6,18,1,128]{3,2,1,0:T(1,128)}, f32[6,18,1,128]{3,2,1,0:T(1,128)S(1)}, u32[]{:S(2)}) copy-start(f32[6,18,1,128]{3,2,1,0:T(1,128)S(1)} %collective-permute-done.15) | copy-start | bytes 165892
  177.3 10.9 %collective-permute-start.17 = (f32[6,18,18,1]{2,1,3,0:T(8,128)S(1)}, f32[6,18,18,1]{2,1,3,0:T(8,128)S(1)}, u32[]{:S(2)}, u32[]{:S(2)}) collective-permute-start(f32[6,18,18,1]{2,1,3,0:T(8,128)S(1)} %copy.132), channel_id=1, source_target_pairs={{0,1},{1,2},{2,3},{4,5},{5,6},{6,7},{8,9},{9,10},{10,11},{12,13},{... | collective-permute-start | bytes 23336 | tf_op jit(solution)/shard_map/ppermute | solution.py:21
  180.3 6.0 %collective-permute-start.16 = (f32[6,18,18,1]{2,1,3,0:T(8,128)S(1)}, f32[6,18,18,1]{2,1,3,0:T(8,128)S(1)}, u32[]{:S(2)}, u32[]{:S(2)}) collective-permute-start(f32[6,18,18,1]{2,1,3,0:T(8,128)S(1)} %copy.131), channel_id=1, source_target_pairs={{1,0},{2,1},{3,2},{5,4},{6,5},{7,6},{9,8},{10,9},{11,10},{13,12},{... | collective-permute-start | bytes 23336 | tf_op jit(solution)/shard_map/ppermute | solution.py:24
  192.8 6.5 %copy-start.4 = (f32[7,18,18,1]{3,2,1,0:T(8,128)S(1)}, f32[7,18,18,1]{3,2,1,0:T(8,128)}, u32[]{:S(2)}) copy-start(f32[7,18,18,1]{3,2,1,0:T(8,128)} %copy.112) | copy-start | bytes 27220
  193.1 6.3 %copy-start.3 = (f32[7,18,18,1]{3,2,1,0:T(8,128)S(1)}, f32[7,18,18,1]{3,2,1,0:T(8,128)}, u32[]{:S(2)}) copy-start(f32[7,18,18,1]{3,2,1,0:T(8,128)} %copy-done.2) | copy-start | bytes 27220
  193.1 6.3 %copy-start.26 = (f32[7,18,1,128]{3,2,1,0:T(1,128)S(1)}, f32[7,18,1,128]{3,2,1,0:T(1,128)}, u32[]{:S(2)}) copy-start(f32[7,18,1,128]{3,2,1,0:T(1,128)} %copy-done.24) | copy-start | bytes 193540
  193.1 6.3 %copy-start.29 = (f32[7,18,1,128]{3,2,1,0:T(1,128)S(1)}, f32[7,18,1,128]{3,2,1,0:T(1,128)}, u32[]{:S(2)}) copy-start(f32[7,18,1,128]{3,2,1,0:T(1,128)} %copy-done.27) | copy-start | bytes 193540
  193.2 34.3 %copy-start.1 = (f32[6,16,16,128]{3,2,1,0:T(8,128)}, f32[6,16,16,128]{3,2,1,0:T(8,128)S(1)}, u32[]{:S(2)}) copy-start(f32[6,16,16,128]{3,2,1,0:T(8,128)S(1)} %fusion.37) | copy-start | bytes 2359300
  193.3 8.4 %collective-permute-start.19 = (f32[6,1,16,128]{3,2,1,0:T(8,128)S(1)}, f32[6,1,16,128]{3,2,1,0:T(8,128)S(1)}, u32[]{:S(2)}, u32[]{:S(2)}) collective-permute-start(f32[6,1,16,128]{3,2,1,0:T(8,128)S(1)} %get-tuple-element.66), channel_id=1, source_target_pairs={{0,16},{16,32},{32,48},{48,64},{64,80},{80,96},{96,112},{112,128},... | collective-permute-start | bytes 147464 | tf_op jit(solution)/shard_map/ppermute | solution.py:21
  197.4 5.4 %collective-permute-start.18 = (f32[6,1,16,128]{3,2,1,0:T(8,128)S(1)}, f32[6,1,16,128]{3,2,1,0:T(8,128)S(1)}, u32[]{:S(2)}, u32[]{:S(2)}) collective-permute-start(f32[6,1,16,128]{3,2,1,0:T(8,128)S(1)} %get-tuple-element.67), channel_id=1, source_target_pairs={{16,0},{32,16},{48,32},{64,48},{80,64},{96,80},{112,96},{128,112},... | collective-permute-start | bytes 147464 | tf_op jit(solution)/shard_map/ppermute | solution.py:24
  202.9 4.2 %collective-permute-start.21 = (f32[6,18,1,128]{3,2,1,0:T(1,128)S(1)}, f32[6,18,1,128]{3,2,1,0:T(1,128)S(1)}, u32[]{:S(2)}, u32[]{:S(2)}) collective-permute-start(f32[6,18,1,128]{3,2,1,0:T(1,128)S(1)} %get-tuple-element.55), channel_id=1, source_target_pairs={{0,4},{4,8},{8,12},{1,5},{5,9},{9,13},{2,6},{6,10},{10,14},{3,7},{... | collective-permute-start | bytes 165896 | tf_op jit(solution)/shard_map/ppermute | solution.py:21
  205.6 5.2 %collective-permute-start.20 = (f32[6,18,1,128]{3,2,1,0:T(1,128)S(1)}, f32[6,18,1,128]{3,2,1,0:T(1,128)S(1)}, u32[]{:S(2)}, u32[]{:S(2)}) collective-permute-start(f32[6,18,1,128]{3,2,1,0:T(1,128)S(1)} %get-tuple-element.56), channel_id=1, source_target_pairs={{4,0},{8,4},{12,8},{5,1},{9,5},{13,9},{6,2},{10,6},{14,10},{7,3},{... | collective-permute-start | bytes 165896 | tf_op jit(solution)/shard_map/ppermute | solution.py:24
  215.7 10.0 %collective-permute-start.23 = (f32[6,18,18,1]{2,1,3,0:T(8,128)S(1)}, f32[6,18,18,1]{2,1,3,0:T(8,128)S(1)}, u32[]{:S(2)}, u32[]{:S(2)}) collective-permute-start(f32[6,18,18,1]{2,1,3,0:T(8,128)S(1)} %copy.134), channel_id=1, source_target_pairs={{0,1},{1,2},{2,3},{4,5},{5,6},{6,7},{8,9},{9,10},{10,11},{12,13},{... | collective-permute-start | bytes 23336 | tf_op jit(solution)/shard_map/ppermute | solution.py:21
  217.9 6.1 %collective-permute-start.22 = (f32[6,18,18,1]{2,1,3,0:T(8,128)S(1)}, f32[6,18,18,1]{2,1,3,0:T(8,128)}, u32[]{:S(2)}, u32[]{:S(2)}) collective-permute-start(f32[6,18,18,1]{2,1,3,0:T(8,128)S(1)} %copy.133), channel_id=1, source_target_pairs={{1,0},{2,1},{3,2},{5,4},{6,5},{7,6},{9,8},{10,9},{11,10},{13,12},{... | collective-permute-start | bytes 23336 | tf_op jit(solution)/shard_map/ppermute | solution.py:24
  233.9 6.6 %collective-permute-start.25 = (f32[16,16,128]{2,1,0:T(8,128)S(1)}, f32[16,16,128]{2,1,0:T(8,128)S(1)}, u32[]{:S(2)}, u32[]{:S(2)}) collective-permute-start(f32[16,16,128]{2,1,0:T(8,128)S(1)} %fusion.81), channel_id=1, source_target_pairs={{4,0},{8,4},{12,8},{5,1},{9,5},{13,9},{6,2},{10,6},{14,10},{7,3},{... | collective-permute-start | bytes 393224 | tf_op jit(solution)/shard_map/ppermute | solution.py:24
  235.2 6.1 %collective-permute-start.24 = (f32[16,16,128]{2,1,0:T(8,128)S(1)}, f32[16,16,128]{2,1,0:T(8,128)S(1)}, u32[]{:S(2)}, u32[]{:S(2)}) collective-permute-start(f32[16,16,128]{2,1,0:T(8,128)S(1)} %fusion.81), channel_id=1, source_target_pairs={{0,4},{4,8},{8,12},{1,5},{5,9},{9,13},{2,6},{6,10},{10,14},{3,7},{... | collective-permute-start | bytes 393224 | tf_op jit(solution)/shard_map/ppermute | solution.py:21
  241.6 8.3 %collective-permute-start.26 = (f32[16,48,16]{2,1,0:T(8,128)S(1)}, f32[16,48,16]{2,1,0:T(8,128)S(1)}, u32[]{:S(2)}, u32[]{:S(2)}) collective-permute-start(f32[16,48,16]{2,1,0:T(8,128)S(1)} %get-tuple-element.72), channel_id=1, source_target_pairs={{0,1},{1,2},{2,3},{4,5},{5,6},{6,7},{8,9},{9,10},{10,11},{12,13},{... | collective-permute-start | bytes 147464 | tf_op jit(solution)/shard_map/ppermute | solution.py:21
  243.1 10.7 %collective-permute-start.27 = (f32[16,48,16]{2,1,0:T(8,128)S(1)}, f32[16,48,16]{2,1,0:T(8,128)S(1)}, u32[]{:S(2)}, u32[]{:S(2)}) collective-permute-start(f32[16,48,16]{2,1,0:T(8,128)S(1)} %get-tuple-element.73), channel_id=1, source_target_pairs={{1,0},{2,1},{3,2},{5,4},{6,5},{7,6},{9,8},{10,9},{11,10},{13,12},{... | collective-permute-start | bytes 147464 | tf_op jit(solution)/shard_map/ppermute | solution.py:24
  255.0 7.5 %collective-permute-start.29 = (f32[16,16,128]{2,1,0:T(8,128)S(1)}, f32[16,16,128]{2,1,0:T(8,128)S(1)}, u32[]{:S(2)}, u32[]{:S(2)}) collective-permute-start(f32[16,16,128]{2,1,0:T(8,128)S(1)} %convolution_bitcast_fusion), channel_id=1, source_target_pairs={{16,0},{32,16},{48,32},{64,48},{80,64},{96,80},{112,96},{128,112},... | collective-permute-start | bytes 393224 | tf_op jit(solution)/shard_map/ppermute | solution.py:24
  259.7 4.0 %collective-permute-start.28 = (f32[16,16,128]{2,1,0:T(8,128)S(1)}, f32[16,16,128]{2,1,0:T(8,128)S(1)}, u32[]{:S(2)}, u32[]{:S(2)}) collective-permute-start(f32[16,16,128]{2,1,0:T(8,128)S(1)} %convolution_bitcast_fusion), channel_id=1, source_target_pairs={{0,16},{16,32},{32,48},{48,64},{64,80},{80,96},{96,112},{112,128},... | collective-permute-start | bytes 393224 | tf_op jit(solution)/shard_map/ppermute | solution.py:21
  (31 other events, 60.1 us)
where the time goes:
time: 269 us; the launch traced here: 265 us
  blocking collectives  79.5 us (30%)
  starting transfers between devices  75.7 us (28%)
  local copies, waits for them, and re-layouts  48.8 us (18%)
  waiting for transfers between devices  32.4 us (12%)
  other arithmetic  22.5 us (8%)
  between operations  4.15 us (2%)
    psum x1, blocking collectives, body(): totals = lax.psum((port_re, port_im), ('gz', 'gy', 'gx'))  79.5 us
    ppermute x15, starting transfers between devices, with_halo(): lax.ppermute(lax.slice_in_dim(block, block.shape[dim] - width, None, axis...  46.9 us
    ppermute x15, starting transfers between devices, with_halo(): lax.ppermute(lax.slice_in_dim(block, 0, width, axis=dim), axis, backward)  28.8 us
    ppermute x15, waiting for transfers between devices, with_halo(): lax.ppermute(lax.slice_in_dim(block, 0, width, axis=dim), axis, backward)  24.9 us
    unnamed x107, local copies, waits for them, and re-layouts  18.8 us
    ppermute x4, local copies, waits for them, and re-layouts, with_halo(): lax.ppermute(lax.slice_in_dim(block, 0, width, axis=dim), axis, backward)  9.09 us
    ppermute x4, local copies, waits for them, and re-layouts, with_halo(): lax.ppermute(lax.slice_in_dim(block, block.shape[dim] - width, None, axis...  8.11 us
    ppermute x15, waiting for transfers between devices, with_halo(): lax.ppermute(lax.slice_in_dim(block, block.shape[dim] - width, None, axis...  7.54 us
  transfers between devices with their start and end apart: 30, of which 11 were waited for; matrix products, arithmetic and copies ran while one was open for 13% of the time, Pallas kernels for 0%

commit v1 on v0

v1 whole, which is shorter than its diff:
```python
import jax
import jax.numpy as jnp
from jax import lax
from jax.experimental import pallas as pl
from jax.experimental.pallas import tpu as pltpu
from jax.sharding import PartitionSpec as P

MU_GAIN = 19.0
KAPPA_GAIN = 2.0
RELAX = 0.8
SENS_GAIN = 0.1
REACH = 16
MESH = pl.DeviceIdType.MESH
AXES = ("gz", "gy", "gx")
F32 = jnp.float32
BF16 = jnp.bfloat16
D = 16
H = 16
L = 128


def plane(index):
    return pl.ds(pl.multiple_of(index * H, H), H)


def tri(value):
    value = jnp.maximum(value, 0)
    return value * (value + 1) // 2


def norm_of(radius, position, length):
    whole = (radius + 1) * (radius + 1)
    return whole - tri(radius - position) - tri(radius - (length - 1 - position))


def make_kernel(sizes):
    nz, ny, nx = sizes["gz"], sizes["gy"], sizes["gx"]
    total = {"gz": nz * D, "gy": ny * H, "gx": nx * L}
    scale = 4.0 / (total["gz"] * total["gy"] * total["gx"])
    flat = ny * nx

    def kernel(fwd_h, adj_h, den_h, lab_h, prt_h, zt, rz, ry, rx,
               adj_o, grad_o, imp_o,
               f, a0, den, lab, prt, a1, a2, t,
               nu, kap, wzm, wzp, wym, wyp, wxm, wxp, al, be, hx, kk, qq, s,
               zs0, ys0, xs0, zr0, yr0, xr0,
               zsf, ysf, xsf, zrf, yrf, xrf,
               zs1, ys1, xs1, zr1, yr1, xr1,
               zs2, ys2, xs2, zr2, yr2, xr2,
               ky, kz, bx, pb, ysF, yrF, zsF, zrF, st, sr, vb, xin,
               ar1, ar2, in_sem, out_sem,
               ss, rs, as1, ar_s1, as2, ar_s2):
        gz, gy, gx = (lax.axis_index(a) for a in AXES)
        pos = {"gz": gz, "gy": gy, "gx": gx}
        here = gy * nx + gx

        def plane_peer(d):
            q = lax.rem(here + d, flat)
            return {"gy": q // nx, "gx": lax.rem(q, nx)}

        def line_peer(d):
            return {"gz": lax.rem(gz + d, nz)}

        barrier = pltpu.get_barrier_semaphore()

        def greet_plane(d, _):
            pl.semaphore_signal(barrier, inc=1, device_id=plane_peer(d), device_id_type=MESH)
            return 0

        def greet_line(d, _):
            pl.semaphore_signal(barrier, inc=1, device_id=line_peer(d), device_id_type=MESH)
            return 0

        lax.fori_loop(1, flat, greet_plane, 0)
        lax.fori_loop(1, nz, greet_line, 0)
        diagonals = [(dz, dx) for dz in (-1, 1) for dx in (-1, 1)]

        def inside(axis, d):
            size = {"gz": nz, "gy": ny, "gx": nx}[axis]
            return pos[axis] < size - 1 if d > 0 else pos[axis] > 0

        for dz, dx in diagonals:
            @pl.when(jnp.logical_and(inside("gz", dz), inside("gx", dx)))
            def _():
                pl.semaphore_signal(barrier, inc=1, device_id={"gz": gz + dz, "gx": gx + dx}, device_id_type=MESH)

        loads = [
            pltpu.make_async_copy(src, dst, in_sem.at[k])
            for k, (src, dst) in enumerate(((den_h, den), (lab_h, lab), (adj_h, a0), (fwd_h, f), (prt_h, prt)))
        ]
        for load in loads:
            load.start()

        def remote(src, dst, slot, where):
            return pltpu.make_async_remote_copy(
                src_ref=src, dst_ref=dst, send_sem=ss.at[slot], recv_sem=rs.at[slot],
                device_id=where, device_id_type=MESH)

        sent = []

        def beside(axis, d, src, dst, slot):
            copy = remote(src, dst, slot, {axis: pos[axis] + d})
            pl.when(inside(axis, d))(copy.start)
            sent.append((inside(axis, d), copy))
            return (inside(axis, -d), copy)

        def arrive(copies):
            for cond, copy in copies:
                pl.when(cond)(copy.wait_recv)

        def exchange(base, zs, zr, ys, yr, xs, xr):
            copies = []
            for axis, src, dst, k in (("gy", ys, yr, 2), ("gx", xs, xr, 4), ("gz", zs, zr, 0)):
                for d in (-1, 1):
                    side = 0 if d < 0 else 1
                    piece = src if axis == "gx" else src.at[side]
                    copies.append(beside(axis, d, piece, dst.at[1 - side], base + k + side))
            return copies

        edges = {axis: (pos[axis] == 0, pos[axis] == {"gz": nz, "gy": ny, "gx": nx}[axis] - 1) for axis in AXES}
        for axis, bufs in (("gz", (zr0, zrf, zr1, zr2, zrF)), ("gy", (yr0, yrf, yr1, yr2, yrF)),
                           ("gx", (xr0, xrf, xr1, xr2, sr))):
            for side in (0, 1):
                @pl.when(edges[axis][side])
                def _():
                    for buf in bufs:
                        buf[side] = jnp.zeros(buf.shape[1:], F32)
                    if axis == "gx":
                        column = lax.rem(lax.broadcasted_iota(jnp.int32, (H, L), 1), 8)
                        xr0[side, 1] = jnp.where(column // 2 == 2, 1.0, 0.0).astype(F32)
                    else:
                        buf = zr0 if axis == "gz" else yr0
                        buf[side, pl.ds(6 * H, H), :] = jnp.ones((H, L), F32)
        for side, dz_ in ((0, 1), (1, 1)):
            for low in (0, 1):
                @pl.when(edges["gz"][low])
                def _():
                    sr[side, 1 + low] = jnp.zeros(sr.shape[2:], F32)

        lane = lax.broadcasted_iota(jnp.int32, (H, L), 1)
        row = lax.broadcasted_iota(jnp.int32, (H, L), 0)

        lane2 = lax.broadcasted_iota(jnp.int32, (H, 2 * L), 1)
        row2 = lax.broadcasted_iota(jnp.int32, (H, 2 * L), 0)
        low4 = lax.rem(lane2, H)
        high4 = lane2 // H
        ry_l = jnp.zeros((H, 2 * L), jnp.int32)
        rz_l = jnp.zeros((H, 2 * L), jnp.int32)
        ry_r = jnp.zeros((H, L), jnp.int32)
        for b in range(H):
            ry_b = ry[gy * H + b]
            rz_b = rz[gz * D + b]
            ry_l = jnp.where(low4 == b, ry_b, ry_l)
            rz_l = jnp.where(high4 == b, rz_b, rz_l)
            ry_r = jnp.where(row == b, ry_b, ry_r)

        def build(k, _):
            shift = (k // D - 1) * D
            p = lax.rem(k, D)
            band_y = jnp.maximum(ry_l + 1 - jnp.abs(low4 - (row2 + shift)), 0)
            ky[plane(k), :] = jnp.where(high4 == p, band_y, 0).astype(F32).astype(BF16)
            band_z = jnp.maximum(rz_l + 1 - jnp.abs(high4 - (p + shift)), 0)
            kz[plane(k), :] = jnp.where(low4 == row2, band_z, 0).astype(F32).astype(BF16)
            return 0

        lax.fori_loop(0, 3 * D, build, 0)
        rx_own = jnp.broadcast_to(rx[pl.ds(gx, 1), :], (H, L))
        rx_low = jnp.broadcast_to(rx[pl.ds(jnp.maximum(gx - 1, 0), 1), :], (H, L))
        rx_high = jnp.broadcast_to(rx[pl.ds(jnp.minimum(gx + 1, nx - 1), 1), :], (H, L))

        def build_x(k, _):
            target = row + k * H
            own = jnp.maximum(rx_own + 1 - jnp.abs(lane - target), 0)
            low = jnp.maximum(rx_low + 1 - jnp.abs(lane - L - target), 0)
            high = jnp.maximum(rx_high + 1 - jnp.abs(lane + L - target), 0)
            bx[plane(k), pl.ds(0, L)] = own.astype(F32).astype(BF16)
            bx[plane(k), pl.ds(L, L)] = jnp.where(lane < L // 2, high, low).astype(F32).astype(BF16)
            return 0

        lax.fori_loop(0, L // H, build_x, 0)
        norm_yx = (norm_of(ry_r, gy * H + row, total["gy"]) * norm_of(rx_own, gx * L + lane, total["gx"])).astype(F32)

        loads[0].wait()
        loads[1].wait()

        def material(z, _):
            density = den[plane(z), :]
            design = jnp.where(lab[plane(z), :] == 2, 1.0, 0.0).astype(F32)
            square = density * density
            cube = square * density
            nu_design = 1.0 / (1.0 + MU_GAIN * cube)
            nu[plane(z), :] = 1.0 - design + design * nu_design
            kap[plane(z), :] = design * KAPPA_GAIN * cube
            gz_i = gz * D + z
            norm_z = norm_of(rz[gz_i], gz_i, total["gz"]).astype(F32)
            inverse = SENS_GAIN / (norm_yx * norm_z)
            nu_slope = -3.0 * MU_GAIN * design * square * nu_design * nu_design
            kk[plane(z), :] = -0.5 * nu_slope * inverse
            qq[plane(z), :] = 3.0 * KAPPA_GAIN * design * square * inverse
            return 0

        lax.fori_loop(0, D, material, 0)

        def faces(z, _):
            v = nu[plane(z), :]
            below = nu[plane(jnp.maximum(z - 1, 0)), :]
            above = nu[plane(jnp.minimum(z + 1, D - 1)), :]
            wzm[plane(z), :] = jnp.where(z > 0, 0.5 * (v + below), 0.0)
            wzp[plane(z), :] = jnp.where(z < D - 1, 0.5 * (v + above), 0.0)
            wym[plane(z), :] = jnp.where(row > 0, 0.5 * (v + pltpu.roll(v, 1, 0)), 0.0)
            wyp[plane(z), :] = jnp.where(row < H - 1, 0.5 * (v + pltpu.roll(v, H - 1, 0)), 0.0)
            wxm[plane(z), :] = jnp.where(lane > 0, 0.5 * (v + pltpu.roll(v, 1, 1)), 0.0)
            wxp[plane(z), :] = jnp.where(lane < L - 1, 0.5 * (v + pltpu.roll(v, L - 1, 1)), 0.0)
            return 0

        lax.fori_loop(0, D, faces, 0)

        def pack(z, tiles, values):
            out = []
            for n, tile in enumerate(tiles):
                group = None
                for c, v in enumerate(values[4 * n:4 * n + 4]):
                    moved = pltpu.roll(v, 2 * c + 1, 1)
                    group = moved if group is None else jnp.where(lane // 2 == c, moved, group)
                group = pltpu.roll(group, z * 8, 1)
                out.append(jnp.where(lane // 8 == z, group, tile))
            return tuple(out)

        def pair(xr, n):
            below = pltpu.roll(xr[0, n], 1, 1)
            above = pltpu.roll(xr[1, n], L - 1, 1)
            return jnp.where(lax.rem(lane, 2) == 0, above, below)

        def unpack(tile, z, count):
            group = pltpu.roll(tile, lax.rem(L - z * 8, L), 1)
            return [pltpu.roll(group, L - 2 * c - 1, 1) for c in range(count)]

        zero = jnp.zeros((H, L), F32)

        def cell_rows(ref, count, first):
            return ref[pl.ds(first, count * D, stride=H), :]

        loads[2].wait()
        for side, z in ((0, 0), (1, D - 1)):
            for c in range(6):
                zs0[side, pl.ds(c * H, H), :] = a0[pl.ds((c * D + z) * H, H), :]
            zs0[side, pl.ds(6 * H, H), :] = nu[pl.ds(z * H, H), :]
            ys0[side, pl.ds(0, 6 * D), :] = cell_rows(a0, 6, side * (H - 1))
            ys0[side, pl.ds(6 * D, D), :] = cell_rows(nu, 1, side * (H - 1))

        def pack0(z, tiles):
            return pack(z, tiles, [a0[plane(c * D + z), :] for c in range(6)] + [nu[plane(z), :]])

        tiles = lax.fori_loop(0, D, pack0, (zero, zero))
        xs0[0] = tiles[0]
        xs0[1] = tiles[1]

        loads[3].wait()
        loads[4].wait()
        for side, z in ((0, 0), (1, D - 1)):
            for c in range(6):
                zsf[side, pl.ds(c * H, H), :] = f[pl.ds((c * D + z) * H, H), :]
            ysf[side] = cell_rows(f, 6, side * (H - 1))

        def packf(z, carry):
            tiles, re, im = carry
            values = [f[plane(c * D + z), :] for c in range(6)]
            mask = prt[plane(z), :].astype(F32)
            return (pack(z, tiles, values), re + mask * values[2], im + mask * values[5])

        tiles, port_re, port_im = lax.fori_loop(0, D, packf, ((zero, zero), zero, zero))
        xsf[0] = tiles[0]
        xsf[1] = tiles[1]
        ar1[here, pl.ds(0, 8), :] = port_re[:8] + port_re[8:]
        ar1[here, pl.ds(8, 8), :] = port_im[:8] + port_im[8:]

        has_diag = [jnp.logical_and(inside("gz", dz), inside("gx", dx)) for dz, dx in diagonals]
        count = flat - 1 + nz - 1
        for cond in has_diag:
            count = count + cond.astype(jnp.int32)
        pl.semaphore_wait(barrier, count)

        got0 = exchange(0, zs0, zr0, ys0, yr0, xs0, xr0)

        def ar1_copy(d):
            return pltpu.make_async_remote_copy(
                src_ref=ar1.at[here], dst_ref=ar1.at[here], send_sem=as1.at[d],
                recv_sem=ar_s1.at[here], device_id=plane_peer(d), device_id_type=MESH)

        def ar1_from(d):
            q = lax.rem(here + d, flat)
            return pltpu.make_async_remote_copy(
                src_ref=ar1.at[q], dst_ref=ar1.at[q], send_sem=as1.at[d],
                recv_sem=ar_s1.at[q], device_id=plane_peer(d), device_id_type=MESH)

        def ar2_copy(d):
            return pltpu.make_async_remote_copy(
                src_ref=ar2.at[gz], dst_ref=ar2.at[gz], send_sem=as2.at[d],
                recv_sem=ar_s2.at[gz], device_id=line_peer(d), device_id_type=MESH)

        def ar2_from(d):
            q = lax.rem(gz + d, nz)
            return pltpu.make_async_remote_copy(
                src_ref=ar2.at[q], dst_ref=ar2.at[q], send_sem=as2.at[d],
                recv_sem=ar_s2.at[q], device_id=line_peer(d), device_id_type=MESH)

        def loop(first, last, action):
            def step(d, _):
                action(d)
                return 0
            lax.fori_loop(first, last, step, 0)

        loop(1, flat, lambda d: ar1_copy(d).start())
        gotf = exchange(6, zsf, zrf, ysf, yrf, xsf, xrf)

        def inner(a, count, z, begin):
            zm = jnp.maximum(z - 1, 0)
            zp = jnp.minimum(z + 1, D - 1)
            w = [ref[plane(z), :] for ref in (wzm, wzp, wym, wyp, wxm, wxp)]
            for c in range(count):
                v = a[plane(c * D + z), :]
                total_ = w[0] * a[plane(c * D + zm), :] + w[1] * a[plane(c * D + zp), :]
                total_ += w[2] * pltpu.roll(v, 1, 0) + w[3] * pltpu.roll(v, H - 1, 0)
                total_ += w[4] * pltpu.roll(v, 1, 1) + w[5] * pltpu.roll(v, L - 1, 1)
                first = begin(c)
                t[plane(c * D + z), :] = total_ if first is None else total_ + first

        def inner1(z, _):
            kappa = kap[plane(z), :]
            inner(a0, 6, z, lambda c: kappa * f[plane(c * D + z), :])
            return 0

        lax.fori_loop(0, D, inner1, 0)

        arrive(got0)
        x0 = [pair(xr0, 0), pair(xr0, 1)]
        outer_x = jnp.logical_or(lane == 0, lane == L - 1)

        hz = []
        hy = []
        for side, z in ((0, 0), (1, D - 1)):
            hz.append(0.5 * (nu[pl.ds(z * H, H), :] + zr0[side, pl.ds(6 * H, H), :]))
            hy.append(0.5 * (cell_rows(nu, 1, side * (H - 1)) + yr0[side, pl.ds(6 * D, D), :]))

        def add_outer(zr, yr, count):
            for side, z in ((0, 0), (1, D - 1)):
                for c in range(count):
                    t[pl.ds((c * D + z) * H, H), :] += hz[side] * zr[side, pl.ds(c * H, H), :]
                for c in range(count):
                    at = pl.ds(c * D * H + side * (H - 1), D, stride=H)
                    t[at, :] = t[at, :] + hy[side] * yr[side, pl.ds(c * D, D), :]

        add_outer(zr0, yr0, 6)
        def diagonal(z, _):
            total_ = wzm[plane(z), :] + wzp[plane(z), :] + wym[plane(z), :] + wyp[plane(z), :]
            v = nu[plane(z), :]
            outside = unpack(x0[1], z, 3)[2]
            face = jnp.where(outer_x, 0.5 * (v + outside), 0.0)
            hx[plane(z), :] = face
            al[plane(z), :] = total_ + wxm[plane(z), :] + wxp[plane(z), :] + face
            return 0

        lax.fori_loop(0, D, diagonal, 0)
        for side, z in ((0, 0), (1, D - 1)):
            al[pl.ds(z * H, H), :] += hz[side]
            at = pl.ds(side * (H - 1), D, stride=H)
            al[at, :] = al[at, :] + hy[side]

        def finish(z, a, tiles_in, count):
            alpha = al[plane(z), :]
            beta = be[plane(z), :]
            face = hx[plane(z), :]
            outside = unpack(tiles_in[0], z, 4) + unpack(tiles_in[1], z, count - 4)
            tt = [t[plane(c * D + z), :] + face * outside[c] for c in range(count)]
            out = [None] * count
            pairs = [(0, 3), (1, 4), (2, 5)] + ([(6, 7)] if count == 8 else [])
            for re, im in pairs:
                out[re] = (1.0 - RELAX) * a[plane(re * D + z), :] + (tt[re] * alpha + tt[im] * beta)
                out[im] = (1.0 - RELAX) * a[plane(im * D + z), :] + (tt[im] * alpha - tt[re] * beta)
            return out

        def sweep1(z, tiles):
            d = al[plane(z), :]
            kappa = kap[plane(z), :]
            weight = RELAX / (d * d + kappa * kappa)
            al[plane(z), :] = d * weight
            be[plane(z), :] = kappa * weight
            out = finish(z, a0, x0, 6)
            mask = prt[plane(z), :].astype(F32)
            out.append(mask * (d * weight))
            out.append(-mask * (kappa * weight))
            for c in range(8):
                a1[plane(c * D + z), :] = out[c]
            return pack(z, tiles, out)

        tiles = lax.fori_loop(0, D, sweep1, (zero, zero))
        xs1[0] = tiles[0]
        xs1[1] = tiles[1]
        for side, z in ((0, 0), (1, D - 1)):
            for c in range(8):
                zs1[side, pl.ds(c * H, H), :] = a1[pl.ds((c * D + z) * H, H), :]
            ys1[side] = cell_rows(a1, 8, side * (H - 1))
        got1 = exchange(12, zs1, zr1, ys1, yr1, xs1, xr1)

        loop(1, flat, lambda d: ar1_from(d).wait_recv())
        part = ar1[0]
        for q in range(1, flat):
            part = part + ar1[q]
        ar2[gz] = part
        loop(1, nz, lambda d: ar2_copy(d).start())

        def inner2(z, _):
            kappa = kap[plane(z), :]

            def begin(c):
                if c < 6:
                    return kappa * f[plane(c * D + z), :]
                return prt[plane(z), :].astype(F32) if c == 6 else None

            inner(a1, 8, z, begin)
            return 0

        lax.fori_loop(0, D, inner2, 0)
        arrive(gotf)
        xf = [pair(xrf, 0), pair(xrf, 1)]
        arrive(got1)
        loop(1, nz, lambda d: ar2_from(d).wait_recv())
        part = ar2[0]
        for q in range(1, nz):
            part = part + ar2[q]
        link_re = scale * jnp.sum(part[:8])
        link_im = scale * jnp.sum(part[8:])
        imp_o[0] = link_re
        imp_o[1] = link_im
        coef_re = 2.0 * (link_re - zt[0])
        coef_im = -2.0 * (link_im - zt[1])
        add_outer(zr1, yr1, 8)
        x1 = [pair(xr1, 0), pair(xr1, 1)]

        def sweep2(z, tile):
            out = finish(z, a1, x1, 8)
            out[2] = out[2] + (coef_re * out[6] - coef_im * out[7])
            out[5] = out[5] + (coef_re * out[7] + coef_im * out[6])
            for c in range(6):
                a2[plane(c * D + z), :] = out[c]
            outside = unpack(xf[0], z, 4) + unpack(xf[1], z, 2)
            share = zero
            for c in range(6):
                term = out[c] * (f[plane(c * D + z), :] - outside[c])
                share = share + term if c < 3 else share - term
            share = jnp.where(outer_x, share, 0.0)
            t[plane(z), :] = share
            return pack(z, (tile,), [share])[0]

        xs2[...] = lax.fori_loop(0, D, sweep2, zero)
        adj_copy = pltpu.make_async_copy(a2, adj_o, out_sem)
        adj_copy.start()
        hz2 = []
        hy2 = []
        for side, z in ((0, 0), (1, D - 1)):
            share = zero
            for c in range(6):
                here_ = pl.ds((c * D + z) * H, H)
                term = a2[here_, :] * (f[here_, :] - zrf[side, pl.ds(c * H, H), :])
                share = share + term if c < 3 else share - term
            zs2[side] = share
            hz2.append(share)
            share = zero
            for c in range(6):
                at = pl.ds(c * D * H + side * (H - 1), D, stride=H)
                term = a2[at, :] * (f[at, :] - yrf[side, pl.ds(c * D, D), :])
                share = share + term if c < 3 else share - term
            ys2[side] = share
            hy2.append(share)
        got2 = exchange(18, zs2, zr2, ys2, yr2, xs2, xr2)

        def sens(z, last):
            zp = jnp.minimum(z + 1, D - 1)
            ez = zero
            ey = zero
            ex = zero
            more = zero
            av = [a2[plane(c * D + z), :] for c in range(6)]
            fv = [f[plane(c * D + z), :] for c in range(6)]
            for c in range(6):
                a, g = av[c], fv[c]
                tz = (a - a2[plane(c * D + zp), :]) * (g - f[plane(c * D + zp), :])
                ty = (a - pltpu.roll(a, H - 1, 0)) * (g - pltpu.roll(g, H - 1, 0))
                tx = (a - pltpu.roll(a, L - 1, 1)) * (g - pltpu.roll(g, L - 1, 1))
                ez = ez + tz if c < 3 else ez - tz
                ey = ey + ty if c < 3 else ey - ty
                ex = ex + tx if c < 3 else ex - tx
                more = more + g * (g + av[(c + 3) % 6])
            ey = jnp.where(row < H - 1, ey, 0.0)
            ex = jnp.where(lane < L - 1, ex, 0.0)
            energy = ez + last + ey + pltpu.roll(ey, 1, 0) + ex + pltpu.roll(ex, 1, 1) + t[plane(z), :]
            s[plane(z), :] = kk[plane(z), :] * energy + qq[plane(z), :] * more
            return ez

        lax.fori_loop(0, D, sens, zero)
        arrive(got2)
        for side, z in ((0, 0), (1, D - 1)):
            at = pl.ds(z * H, H)
            s[at, :] += kk[at, :] * (hz2[side] + zr2[side])
            at = pl.ds(side * (H - 1), D, stride=H)
            s[at, :] = s[at, :] + kk[at, :] * (hy2[side] + yr2[side])
        below = pltpu.roll(xr2[0], 1, 1)
        above = pltpu.roll(xr2[1], L - 1, 1)
        x2 = jnp.where(lax.rem(lane, 2) == 0, above, below)

        def split(v):
            high = v.astype(BF16)
            return high, (v - high.astype(F32)).astype(BF16)

        def add_x(z, _):
            outside = unpack(x2, z, 1)[0]
            v = s[plane(z), :] + kk[plane(z), :] * jnp.where(outer_x, outside, 0.0)
            high, low = split(v)
            vb[plane(z), pl.ds(0, L)] = high
            vb[plane(z), pl.ds(L, L)] = low
            return 0

        lax.fori_loop(0, D, add_x, 0)

        def band(matrix, dst_low, dst_own, dst_high):
            for n, dst in ((0, dst_low), (2, dst_high), (1, dst_own)):
                both = jnp.dot(matrix[pl.ds(n * D * H, D * H), :], vb[...], preferred_element_type=F32)
                dst[...] = both[:, :L] + both[:, L:]

        band(ky, ysF.at[0], pb, ysF.at[1])
        gotF = []
        for side, d in ((0, -1), (1, 1)):
            gotF.append(beside("gy", d, ysF.at[side], yrF.at[1 - side], 24 + side))
        arrive(gotF)

        def add_y(z, _):
            v = pb[plane(z), :] + yrF[0, plane(z), :] + yrF[1, plane(z), :]
            high, low = split(v)
            vb[plane(z), pl.ds(0, L)] = high
            vb[plane(z), pl.ds(L, L)] = low
            return 0

        lax.fori_loop(0, D, add_y, 0)

        band(kz, zsF.at[0], pb, zsF.at[1])
        gotZ = []
        for side, d in ((0, -1), (1, 1)):
            gotZ.append(beside("gz", d, zsF.at[side], zrF.at[1 - side], 26 + side))

        def strips(src, n):
            for half in range(2):
                def step(p, tiles):
                    v = src[plane(p + 8 * half), :]
                    out = []
                    for side in (0, 1):
                        moved = pltpu.roll(v, lax.rem(p * REACH + side * REACH, L), 1)
                        out.append(jnp.where(lane // REACH == p, moved, tiles[side]))
                    return tuple(out)
                tiles = lax.fori_loop(0, 8, step, (zero, zero))
                for side in (0, 1):
                    st[side, n, half] = tiles[side]

        strips(zsF.at[0], 1)
        strips(zsF.at[1], 2)
        strips(pb, 0)
        gotX = []
        for side, dx in ((0, -1), (1, 1)):
            for n, dz in ((1, -1), (2, 1)):
                go = jnp.logical_and(inside("gx", dx), inside("gz", dz))
                come = jnp.logical_and(inside("gx", -dx), inside("gz", -dz))
                copy = remote(st.at[side, n], sr.at[1 - side, 3 - n], 28 + side * 3 + n,
                              {"gz": gz + dz, "gx": gx + dx})
                pl.when(go)(copy.start)
                sent.append((go, copy))
                gotX.append((come, copy))
            gotX.append(beside("gx", dx, st.at[side, 0], sr.at[1 - side, 0], 28 + side * 3))
        arrive(gotZ)
        arrive(gotX)
        cols = [[sr[side, 0, half] + sr[side, 1, half] + sr[side, 2, half] for half in range(2)] for side in (0, 1)]
        for half in range(2):
            def add_z(p, _):
                at = plane(p + 8 * half)
                v = pb[at, :] + zrF[0, at, :] + zrF[1, at, :]
                back = lax.rem(L - p * REACH, L)
                low = pltpu.roll(cols[0][half], lax.rem(back + L - REACH, L), 1)
                high = pltpu.roll(cols[1][half], back, 1)
                for k, part_ in enumerate((v, jnp.where(lane < L // 2, high, low))):
                    big, small = split(part_)
                    xin[at, pl.ds(k * L, L)] = big
                    xin[plane(p + 8 * half + D), pl.ds(k * L, L)] = small
                return 0
            lax.fori_loop(0, 8, add_z, 0)
        both = lax.dot_general(xin[...], bx[...], (((1,), (1,)), ((), ())), preferred_element_type=F32)
        grad_o[...] = both[:D * H] + both[D * H:]

        for cond, copy in sent:
            pl.when(cond)(copy.wait_send)
        loop(1, flat, lambda d: ar1_copy(d).wait_send())
        loop(1, nz, lambda d: ar2_copy(d).wait_send())
        adj_copy.wait()

    return kernel


def solution(mesh):
    sizes = dict(mesh.shape)
    nz, ny, nx = (sizes[a] for a in AXES)
    rows = D * H
    vm = lambda *shape: pltpu.VMEM(shape, F32)
    field = vm(rows, L)

    def halo(planes, tiles):
        y = vm(2, planes * D, L)
        z = vm(2, planes * H, L)
        return [z, y, vm(tiles, H, L), z, y, vm(2, tiles, H, L)]

    scratch = [
        vm(6 * rows, L), vm(6 * rows, L), field, pltpu.VMEM((rows, L), jnp.int32), pltpu.VMEM((rows, L), jnp.int32),
        vm(8 * rows, L), vm(6 * rows, L), vm(8 * rows, L),
    ] + [field] * 14 + halo(7, 2) + halo(6, 2) + halo(8, 2) + [
        vm(2, H, L), vm(2, D, L), vm(H, L), vm(2, H, L), vm(2, D, L), vm(2, H, L),
        pltpu.VMEM((3 * rows, 2 * L), BF16), pltpu.VMEM((3 * rows, 2 * L), BF16), pltpu.VMEM((L, 2 * L), BF16),
        field, vm(2, rows, L), vm(2, rows, L), vm(2, rows, L), vm(2, rows, L),
        vm(2, 3, 2, H, L), vm(2, 3, 2, H, L),
        pltpu.VMEM((rows, 2 * L), BF16), pltpu.VMEM((2 * rows, 2 * L), BF16),
        vm(ny * nx, H, L), vm(nz, H, L),
        pltpu.SemaphoreType.DMA((5,)), pltpu.SemaphoreType.DMA,
        pltpu.SemaphoreType.DMA((34,)), pltpu.SemaphoreType.DMA((34,)),
        pltpu.SemaphoreType.DMA((ny * nx,)), pltpu.SemaphoreType.DMA((ny * nx,)),
        pltpu.SemaphoreType.DMA((nz,)), pltpu.SemaphoreType.DMA((nz,)),
    ]
    hbm = pl.BlockSpec(memory_space=pl.ANY)
    smem = pl.BlockSpec(memory_space=pltpu.SMEM)
    vmem = pl.BlockSpec(memory_space=pltpu.VMEM)
    call = pl.pallas_call(
        make_kernel(sizes),
        out_shape=(
            jax.ShapeDtypeStruct((6 * rows, L), F32),
            jax.ShapeDtypeStruct((rows, L), F32),
            jax.ShapeDtypeStruct((2,), F32),
        ),
        in_specs=[hbm] * 5 + [smem] * 3 + [vmem],
        out_specs=(hbm, vmem, smem),
        scratch_shapes=scratch,
        compiler_params=pltpu.CompilerParams(
            collective_id=0, has_side_effects=True, vmem_limit_bytes=48 * 2**20),
    )

    def body(forward, adjoint_prev, density, labels, ports, z_target, radius_z, radius_y, radius_x):
        adjoint, gradient, impedance = call(
            forward.reshape(6 * rows, L), adjoint_prev.reshape(6 * rows, L), density.reshape(rows, L),
            labels.reshape(rows, L), ports.reshape(rows, L), z_target, radius_z, radius_y,
            radius_x.reshape(nx, L))
        return adjoint.reshape(6, D, H, L), gradient.reshape(D, H, L), impedance

    in_specs = (P(None, *AXES),) * 2 + (P(*AXES),) * 3 + (P(),) * 4
    out_specs = (P(None, *AXES), P(*AXES), P())
    return jax.shard_map(body, mesh=mesh, in_specs=in_specs, out_specs=out_specs, check_vma=False)
```

time: 269 us -> 68.4 us (0.25); the launches traced: 265 us -> 68.1 us
  blocking collectives: 79.5 us -> 0 us
  starting transfers between devices: 75.7 us -> 0 us
  Pallas kernels: 0 us -> 59.7 us
  local copies, waits for them, and re-layouts: 48.8 us -> 7.71 us
  waiting for transfers between devices: 32.4 us -> 0 us
  other arithmetic: 22.5 us -> 0 us
  between operations: 4.15 us -> 0.68 us
    psum x1 -> x0, blocking collectives: 79.5 us -> none  [body(): totals = lax.psum((port_re, port_im), ('gz', 'gy', 'gx'))]
    ppermute x30 -> x0, starting transfers between devices: 75.7 us -> none  [the longest x15 46.9 us: with_halo(): lax.ppermute(lax.slice_in_dim(block, block.shape[dim] - width, None, axis...]
    pallas_call x0 -> x1, Pallas kernels: none -> 59.7 us  [body(): call(forward.reshape(6 * rows, L), adjoint_prev.reshape(6 * rows, L), den...]
    ppermute x30 -> x0, waiting for transfers between devices: 32.4 us -> none  [the longest x15 24.9 us: with_halo(): lax.ppermute(lax.slice_in_dim(block, 0, width, axis=dim), axis, backward)]
    ppermute x8 -> x0, local copies, waits for them, and re-layouts: 17.2 us -> none  [the longest x4 9.09 us: with_halo(): lax.ppermute(lax.slice_in_dim(block, 0, width, axis=dim), axis, backward)]
    sub x11 -> x0, other arithmetic: 13.1 us -> none  [the longest x2 4.49 us: sensitivity(): diff_fwd = forward - fwd_near]
    slice x12 -> x0, local copies, waits for them, and re-layouts: 12.8 us -> none  [the longest x5 7.35 us: with_halo(): lax.slice_in_dim(block, 0, width, axis=dim)]
    unnamed x107 -> x21, local copies, waits for them, and re-layouts: 18.8 us -> 7.71 us
  transfers between devices with their start and end apart: 30 -> 0, of which waited for: 11 -> 0; matrix products, arithmetic and copies ran while one was open for 13% -> 0% of each run, Pallas kernels for 0% -> 0%
where the time goes in v1:
time: 68.4 us; the launch traced here: 68.1 us
  Pallas kernels  59.7 us (87%)
  local copies, waits for them, and re-layouts  7.71 us (11%)
    pallas_call x1, Pallas kernels, body(): call(forward.reshape(6 * rows, L), adjoint_prev.reshape(6 * rows, L), den...  59.7 us
    unnamed x21, local copies, waits for them, and re-layouts  7.71 us

profile of v1, /device:TPU:1, one launch (start us, length us, event | category | flops | bytes accessed | tf_op | source)
XLA Modules:
  0.0 68.1 jit_solution(7571362014085872527)
XLA Ops:
  0.6 0.0 copy-start.8
  0.6 0.0 copy-start.5
  0.7 0.0 copy-start.6
  0.7 0.0 copy-start.7
  0.7 0.6 copy-done.8
  1.3 0.0 copy-done.5
  1.3 0.0 copy-done.6
  1.3 0.0 copy-done.7
  1.3 0.0 copy-start
  1.4 1.1 %copy-done = f32[6,16,16,128]{3,2,1,0:T(8,128)S(1)} copy-done((f32[6,16,16,128]{3,2,1,0:T(8,128)S(1)}, f32[6,16,16,128]{3,2,1,0:T(8,128)}, u32[]{:S(2)}) %copy-start) | copy-done | bytes 786456
  2.5 0.0 copy-start.1
  2.5 1.1 %copy-done.1 = f32[6,16,16,128]{3,2,1,0:T(8,128)S(1)} copy-done((f32[6,16,16,128]{3,2,1,0:T(8,128)S(1)}, f32[6,16,16,128]{3,2,1,0:T(8,128)}, u32[]{:S(2)}) %copy-start.1) | copy-done | bytes 786456
  3.6 0.0 copy-start.2
  3.6 0.9 %copy-done.2 = f32[16,16,128]{2,1,0:T(8,128)S(1)} copy-done((f32[16,16,128]{2,1,0:T(8,128)S(1)}, f32[16,16,128]{2,1,0:T(8,128)}, u32[]{:S(2)}) %copy-start.2) | copy-done | bytes 131096
  4.5 0.0 copy-start.3
  4.5 0.9 %copy-done.3 = s32[16,16,128]{2,1,0:T(8,128)S(1)} copy-done((s32[16,16,128]{2,1,0:T(8,128)S(1)}, s32[16,16,128]{2,1,0:T(8,128)}, u32[]{:S(2)}) %copy-start.3) | copy-done | bytes 131096
  5.4 0.0 copy-start.4
  5.4 0.9 %copy-done.4 = s32[16,16,128]{2,1,0:T(8,128)S(1)} copy-done((s32[16,16,128]{2,1,0:T(8,128)S(1)}, s32[16,16,128]{2,1,0:T(8,128)}, u32[]{:S(2)}) %copy-start.4) | copy-done | bytes 131096
  6.3 59.7 %shard_map.112 = (f32[1536,128]{1,0:T(8,128)S(1)}, f32[256,128]{1,0:T(8,128)S(1)}, f32[2]{0:T(128)S(1)}) custom-call(f32[1536,128]{1,0:T(8,128)S(1)} %bitcast.9, f32[1536,128]{1,0:T(8,128)S(1)} %bitcast.10, f32[256,128]{1,0:T(8,128)S(1)} %bitcast.12, s32[256,128]{1,0:T(8,128)S(1)} %bitcast.13, s32[256,128]{1,0:T(8,128)S(1)} %bitcast.14, f32[2]{0:T(128)S(1)} %copy-done.7, ...), custom_call_target="tpu_custom_call" | custom-call | tf_op jit(solution)/shard_map/pallas_call | solution.py:650
  66.1 0.9 %copy.15 = f32[6,16,16,128]{3,2,1,0:T(8,128)} copy(f32[6,16,16,128]{3,2,1,0:T(8,128)S(1)} %bitcast.8) | data formatting | bytes 1572864
  67.0 0.7 copy.16
  67.6 0.5 copy.17
Async XLA Ops:
  0.6 0.7 copy-start.8
  0.6 0.7 %copy-start.5 = (s32[512]{0:T(512)S(1)}, s32[512]{0:T(512)}, u32[]{:S(2)}) copy-start(s32[512]{0:T(512)} %param.17) | copy-start | bytes 6148
  0.7 0.7 %copy-start.6 = (s32[256]{0:T(256)S(1)}, s32[256]{0:T(256)}, u32[]{:S(2)}) copy-start(s32[256]{0:T(256)} %rz.1) | copy-start | bytes 3076
  0.7 0.7 %copy-start.7 = (f32[2]{0:T(128)S(1)}, f32[2]{0:T(128)}, u32[]{:S(2)}) copy-start(f32[2]{0:T(128)} %zt.1) | copy-start | bytes 28
  1.3 1.1 %copy-start = (f32[6,16,16,128]{3,2,1,0:T(8,128)S(1)}, f32[6,16,16,128]{3,2,1,0:T(8,128)}, u32[]{:S(2)}) copy-start(f32[6,16,16,128]{3,2,1,0:T(8,128)} %param.9) | copy-start | bytes 2359300
  2.5 1.1 %copy-start.1 = (f32[6,16,16,128]{3,2,1,0:T(8,128)S(1)}, f32[6,16,16,128]{3,2,1,0:T(8,128)}, u32[]{:S(2)}) copy-start(f32[6,16,16,128]{3,2,1,0:T(8,128)} %param.10) | copy-start | bytes 2359300
  3.6 0.9 %copy-start.2 = (f32[16,16,128]{2,1,0:T(8,128)S(1)}, f32[16,16,128]{2,1,0:T(8,128)}, u32[]{:S(2)}) copy-start(f32[16,16,128]{2,1,0:T(8,128)} %param.11) | copy-start | bytes 393220
  4.5 0.9 %copy-start.3 = (s32[16,16,128]{2,1,0:T(8,128)S(1)}, s32[16,16,128]{2,1,0:T(8,128)}, u32[]{:S(2)}) copy-start(s32[16,16,128]{2,1,0:T(8,128)} %param.12) | copy-start | bytes 393220
  5.4 0.9 %copy-start.4 = (s32[16,16,128]{2,1,0:T(8,128)S(1)}, s32[16,16,128]{2,1,0:T(8,128)}, u32[]{:S(2)}) copy-start(s32[16,16,128]{2,1,0:T(8,128)} %param.13) | copy-start | bytes 393220

commit v2 on v1

--- a/solution.py
+++ b/solution.py
@@ -10,6 +10,8 @@
 RELAX = 0.8
 SENS_GAIN = 0.1
 REACH = 16
+CORES = 2
+WIDTH = dict(add_x=16, add_y=16, add_z=8, build=4, build_x=4, diagonal=16, faces=16, inner1=16, inner2=16, material=16, pack0=16, packf=16, sens=16, step=8, sweep1=16, sweep2=16, join=16, answer=16)
 MESH = pl.DeviceIdType.MESH
 AXES = ("gz", "gy", "gx")
 F32 = jnp.float32
@@ -20,7 +22,33 @@
 
 
 def plane(index):
+    if isinstance(index, int):
+        return pl.ds(index * H, H)
     return pl.ds(pl.multiple_of(index * H, H), H)
+
+
+def each(count, step, carry, width):
+    if width == count:
+        for k in range(count):
+            carry = step(k, carry)
+        return carry
+
+    def group(g, carry):
+        for k in range(width):
+            carry = step(g * width + k, carry)
+        return carry
+
+    return lax.fori_loop(0, count // width, group, carry)
+
+
+def mod(a, b):
+    return a % b if isinstance(a, int) else lax.rem(a, b)
+
+
+def clamp(value):
+    if isinstance(value, int):
+        return min(max(value, 0), D - 1)
+    return jnp.clip(value, 0, D - 1)
 
 
 def tri(value):
@@ -37,7 +65,6 @@
     nz, ny, nx = sizes["gz"], sizes["gy"], sizes["gx"]
     total = {"gz": nz * D, "gy": ny * H, "gx": nx * L}
     scale = 4.0 / (total["gz"] * total["gy"] * total["gx"])
-    flat = ny * nx
 
     def kernel(fwd_h, adj_h, den_h, lab_h, prt_h, zt, rz, ry, rx,
                adj_o, grad_o, imp_o,
@@ -48,41 +75,39 @@
                zs1, ys1, xs1, zr1, yr1, xr1,
                zs2, ys2, xs2, zr2, yr2, xr2,
                ky, kz, bx, pb, ysF, yrF, zsF, zrF, st, sr, vb, xin,
-               ar1, ar2, in_sem, out_sem,
-               ss, rs, as1, ar_s1, as2, ar_s2):
+               sum_core, sum_x, sum_y, sum_z, in_sem, out_sem, ss, rs,
+               ss_core, rs_core, ss_x, rs_x, ss_y, rs_y, ss_z, rs_z):
+        sums = {"core": sum_core, "gx": sum_x, "gy": sum_y, "gz": sum_z}
+        sum_ss = {"core": ss_core, "gx": ss_x, "gy": ss_y, "gz": ss_z}
+        sum_rs = {"core": rs_core, "gx": rs_x, "gy": rs_y, "gz": rs_z}
         gz, gy, gx = (lax.axis_index(a) for a in AXES)
         pos = {"gz": gz, "gy": gy, "gx": gx}
-        here = gy * nx + gx
-
-        def plane_peer(d):
-            q = lax.rem(here + d, flat)
-            return {"gy": q // nx, "gx": lax.rem(q, nx)}
-
-        def line_peer(d):
-            return {"gz": lax.rem(gz + d, nz)}
-
-        barrier = pltpu.get_barrier_semaphore()
-
-        def greet_plane(d, _):
-            pl.semaphore_signal(barrier, inc=1, device_id=plane_peer(d), device_id_type=MESH)
-            return 0
-
-        def greet_line(d, _):
-            pl.semaphore_signal(barrier, inc=1, device_id=line_peer(d), device_id_type=MESH)
-            return 0
-
-        lax.fori_loop(1, flat, greet_plane, 0)
-        lax.fori_loop(1, nz, greet_line, 0)
-        diagonals = [(dz, dx) for dz in (-1, 1) for dx in (-1, 1)]
+        core = lax.rem(gz, CORES)
 
         def inside(axis, d):
             size = {"gz": nz, "gy": ny, "gx": nx}[axis]
             return pos[axis] < size - 1 if d > 0 else pos[axis] > 0
 
-        for dz, dx in diagonals:
-            @pl.when(jnp.logical_and(inside("gz", dz), inside("gx", dx)))
+        stages = {
+            "core": (CORES, lambda d: {"gz": gz - core + lax.rem(core + d, CORES)}, core),
+            "gx": (nx, lambda d: {"gx": lax.rem(gx + d, nx)}, gx),
+            "gy": (ny, lambda d: {"gy": lax.rem(gy + d, ny)}, gy),
+            "gz": (nz // CORES, lambda d: {"gz": lax.rem(gz + CORES * d, nz)}, gz // CORES),
+        }
+        barrier = pltpu.get_barrier_semaphore()
+        others = [(dz, dx, jnp.logical_and(inside("gz", dz), inside("gx", dx))) for dz in (-1, 1) for dx in (-1, 1)]
+        others += [(dz, 0, jnp.logical_and(inside("gz", dz), (core == 0) if dz < 0 else (core == CORES - 1)))
+                   for dz in (-1, 1)]
+        expected = 0
+        for members, peer, _ in stages.values():
+            for d in range(1, members):
+                pl.semaphore_signal(barrier, inc=1, device_id=peer(d), device_id_type=MESH)
+                expected += 1
+        for dz, dx, cond in others:
+            @pl.when(cond)
             def _():
                 pl.semaphore_signal(barrier, inc=1, device_id={"gz": gz + dz, "gx": gx + dx}, device_id_type=MESH)
+            expected = expected + cond.astype(jnp.int32)
 
         loads = [
             pltpu.make_async_copy(src, dst, in_sem.at[k])
@@ -163,7 +188,7 @@
             kz[plane(k), :] = jnp.where(low4 == row2, band_z, 0).astype(F32).astype(BF16)
             return 0
 
-        lax.fori_loop(0, 3 * D, build, 0)
+        each(3 * D, build, 0, WIDTH['build'])
         rx_own = jnp.broadcast_to(rx[pl.ds(gx, 1), :], (H, L))
         rx_low = jnp.broadcast_to(rx[pl.ds(jnp.maximum(gx - 1, 0), 1), :], (H, L))
         rx_high = jnp.broadcast_to(rx[pl.ds(jnp.minimum(gx + 1, nx - 1), 1), :], (H, L))
@@ -177,7 +202,7 @@
             bx[plane(k), pl.ds(L, L)] = jnp.where(lane < L // 2, high, low).astype(F32).astype(BF16)
             return 0
 
-        lax.fori_loop(0, L // H, build_x, 0)
+        each(L // H, build_x, 0, WIDTH['build_x'])
         norm_yx = (norm_of(ry_r, gy * H + row, total["gy"]) * norm_of(rx_own, gx * L + lane, total["gx"])).astype(F32)
 
         loads[0].wait()
@@ -199,12 +224,12 @@
             qq[plane(z), :] = 3.0 * KAPPA_GAIN * design * square * inverse
             return 0
 
-        lax.fori_loop(0, D, material, 0)
+        each(D, material, 0, WIDTH['material'])
 
         def faces(z, _):
             v = nu[plane(z), :]
-            below = nu[plane(jnp.maximum(z - 1, 0)), :]
-            above = nu[plane(jnp.minimum(z + 1, D - 1)), :]
+            below = nu[plane(clamp(z - 1)), :]
+            above = nu[plane(clamp(z + 1)), :]
             wzm[plane(z), :] = jnp.where(z > 0, 0.5 * (v + below), 0.0)
             wzp[plane(z), :] = jnp.where(z < D - 1, 0.5 * (v + above), 0.0)
             wym[plane(z), :] = jnp.where(row > 0, 0.5 * (v + pltpu.roll(v, 1, 0)), 0.0)
@@ -213,17 +238,13 @@
             wxp[plane(z), :] = jnp.where(lane < L - 1, 0.5 * (v + pltpu.roll(v, L - 1, 1)), 0.0)
             return 0
 
-        lax.fori_loop(0, D, faces, 0)
+        each(D, faces, 0, WIDTH['faces'])
 
         def pack(z, tiles, values):
-            out = []
-            for n, tile in enumerate(tiles):
-                group = None
-                for c, v in enumerate(values[4 * n:4 * n + 4]):
-                    moved = pltpu.roll(v, 2 * c + 1, 1)
-                    group = moved if group is None else jnp.where(lane // 2 == c, moved, group)
-                group = pltpu.roll(group, z * 8, 1)
-                out.append(jnp.where(lane // 8 == z, group, tile))
+            out = list(tiles)
+            for c, v in enumerate(values):
+                moved = pltpu.roll(v, (z * 8 + 2 * (c % 4) + 1) % L, 1)
+                out[c // 4] = jnp.where(lane // 2 == z * 4 + c % 4, moved, out[c // 4])
             return tuple(out)
 
         def pair(xr, n):
@@ -231,9 +252,8 @@
             above = pltpu.roll(xr[1, n], L - 1, 1)
             return jnp.where(lax.rem(lane, 2) == 0, above, below)
 
-        def unpack(tile, z, count):
-            group = pltpu.roll(tile, lax.rem(L - z * 8, L), 1)
-            return [pltpu.roll(group, L - 2 * c - 1, 1) for c in range(count)]
+        def unpack(tile, z, count, first=0):
+            return [pltpu.roll(tile, (-z * 8 - 2 * c - 1) % L, 1) for c in range(first, first + count)]
 
         zero = jnp.zeros((H, L), F32)
 
@@ -251,7 +271,7 @@
         def pack0(z, tiles):
             return pack(z, tiles, [a0[plane(c * D + z), :] for c in range(6)] + [nu[plane(z), :]])
 
-        tiles = lax.fori_loop(0, D, pack0, (zero, zero))
+        tiles = each(D, pack0, (zero, zero), WIDTH['pack0'])
         xs0[0] = tiles[0]
         xs0[1] = tiles[1]
 
@@ -268,54 +288,43 @@
             mask = prt[plane(z), :].astype(F32)
             return (pack(z, tiles, values), re + mask * values[2], im + mask * values[5])
 
-        tiles, port_re, port_im = lax.fori_loop(0, D, packf, ((zero, zero), zero, zero))
+        tiles, port_re, port_im = each(D, packf, ((zero, zero), zero, zero), WIDTH['packf'])
         xsf[0] = tiles[0]
         xsf[1] = tiles[1]
-        ar1[here, pl.ds(0, 8), :] = port_re[:8] + port_re[8:]
-        ar1[here, pl.ds(8, 8), :] = port_im[:8] + port_im[8:]
-
-        has_diag = [jnp.logical_and(inside("gz", dz), inside("gx", dx)) for dz, dx in diagonals]
-        count = flat - 1 + nz - 1
-        for cond in has_diag:
-            count = count + cond.astype(jnp.int32)
-        pl.semaphore_wait(barrier, count)
-
+        port_sum = jnp.concatenate(
+            [jnp.sum(port_re, axis=0, keepdims=True), jnp.sum(port_im, axis=0, keepdims=True)], axis=0)
+
+        pl.semaphore_wait(barrier, expected)
         got0 = exchange(0, zs0, zr0, ys0, yr0, xs0, xr0)
 
-        def ar1_copy(d):
+        def sum_copy(stage, d, arriving):
+            members, peer, slot = stages[stage]
+            at = lax.rem(slot + d, members) if arriving else slot
+            ref = sums[stage].at[at]
             return pltpu.make_async_remote_copy(
-                src_ref=ar1.at[here], dst_ref=ar1.at[here], send_sem=as1.at[d],
-                recv_sem=ar_s1.at[here], device_id=plane_peer(d), device_id_type=MESH)
-
-        def ar1_from(d):
-            q = lax.rem(here + d, flat)
-            return pltpu.make_async_remote_copy(
-                src_ref=ar1.at[q], dst_ref=ar1.at[q], send_sem=as1.at[d],
-                recv_sem=ar_s1.at[q], device_id=plane_peer(d), device_id_type=MESH)
-
-        def ar2_copy(d):
-            return pltpu.make_async_remote_copy(
-                src_ref=ar2.at[gz], dst_ref=ar2.at[gz], send_sem=as2.at[d],
-                recv_sem=ar_s2.at[gz], device_id=line_peer(d), device_id_type=MESH)
-
-        def ar2_from(d):
-            q = lax.rem(gz + d, nz)
-            return pltpu.make_async_remote_copy(
-                src_ref=ar2.at[q], dst_ref=ar2.at[q], send_sem=as2.at[d],
-                recv_sem=ar_s2.at[q], device_id=line_peer(d), device_id_type=MESH)
-
-        def loop(first, last, action):
-            def step(d, _):
-                action(d)
-                return 0
-            lax.fori_loop(first, last, step, 0)
-
-        loop(1, flat, lambda d: ar1_copy(d).start())
-        gotf = exchange(6, zsf, zrf, ysf, yrf, xsf, xrf)
+                src_ref=ref, dst_ref=ref, send_sem=sum_ss[stage].at[d], recv_sem=sum_rs[stage].at[at],
+                device_id=peer(d), device_id_type=MESH)
+
+        def sum_start(stage, value):
+            members, _, slot = stages[stage]
+            sums[stage][slot] = value
+            for d in range(1, members):
+                sum_copy(stage, d, False).start()
+
+        def sum_finish(stage):
+            members = stages[stage][0]
+            for d in range(1, members):
+                sum_copy(stage, d, True).wait_recv()
+            value = sums[stage][0]
+            for q in range(1, members):
+                value = value + sums[stage][q]
+            return value
+
+        sum_start("core", port_sum)
 
         def inner(a, count, z, begin):
-            zm = jnp.maximum(z - 1, 0)
-            zp = jnp.minimum(z + 1, D - 1)
+            zm = clamp(z - 1)
+            zp = clamp(z + 1)
             w = [ref[plane(z), :] for ref in (wzm, wzp, wym, wyp, wxm, wxp)]
             for c in range(count):
                 v = a[plane(c * D + z), :]
@@ -330,7 +339,9 @@
             inner(a0, 6, z, lambda c: kappa * f[plane(c * D + z), :])
             return 0
 
-        lax.fori_loop(0, D, inner1, 0)
+        each(D, inner1, 0, WIDTH['inner1'])
+        sum_start("gx", sum_finish("core"))
+        gotf = exchange(6, zsf, zrf, ysf, yrf, xsf, xrf)
 
         arrive(got0)
         x0 = [pair(xr0, 0), pair(xr0, 1)]
@@ -354,13 +365,13 @@
         def diagonal(z, _):
             total_ = wzm[plane(z), :] + wzp[plane(z), :] + wym[plane(z), :] + wyp[plane(z), :]
             v = nu[plane(z), :]
-            outside = unpack(x0[1], z, 3)[2]
+            outside = unpack(x0[1], z, 1, 2)[0]
             face = jnp.where(outer_x, 0.5 * (v + outside), 0.0)
             hx[plane(z), :] = face
             al[plane(z), :] = total_ + wxm[plane(z), :] + wxp[plane(z), :] + face
             return 0
 
-        lax.fori_loop(0, D, diagonal, 0)
+        each(D, diagonal, 0, WIDTH['diagonal'])
         for side, z in ((0, 0), (1, D - 1)):
             al[pl.ds(z * H, H), :] += hz[side]
             at = pl.ds(side * (H - 1), D, stride=H)
@@ -393,7 +404,7 @@
                 a1[plane(c * D + z), :] = out[c]
             return pack(z, tiles, out)
 
-        tiles = lax.fori_loop(0, D, sweep1, (zero, zero))
+        tiles = each(D, sweep1, (zero, zero), WIDTH['sweep1'])
         xs1[0] = tiles[0]
         xs1[1] = tiles[1]
         for side, z in ((0, 0), (1, D - 1)):
@@ -402,12 +413,7 @@
             ys1[side] = cell_rows(a1, 8, side * (H - 1))
         got1 = exchange(12, zs1, zr1, ys1, yr1, xs1, xr1)
 
-        loop(1, flat, lambda d: ar1_from(d).wait_recv())
-        part = ar1[0]
-        for q in range(1, flat):
-            part = part + ar1[q]
-        ar2[gz] = part
-        loop(1, nz, lambda d: ar2_copy(d).start())
+        sum_start("gy", sum_finish("gx"))
 
         def inner2(z, _):
             kappa = kap[plane(z), :]
@@ -420,107 +426,113 @@
             inner(a1, 8, z, begin)
             return 0
 
-        lax.fori_loop(0, D, inner2, 0)
+        each(D, inner2, 0, WIDTH['inner2'])
+        sum_start("gz", sum_finish("gy"))
         arrive(gotf)
         xf = [pair(xrf, 0), pair(xrf, 1)]
         arrive(got1)
-        loop(1, nz, lambda d: ar2_from(d).wait_recv())
-        part = ar2[0]
-        for q in range(1, nz):
-            part = part + ar2[q]
-        link_re = scale * jnp.sum(part[:8])
-        link_im = scale * jnp.sum(part[8:])
+        add_outer(zr1, yr1, 8)
+        x1 = [pair(xr1, 0), pair(xr1, 1)]
+
+        def shares(answers, near):
+            main = None
+            for c in range(6):
+                term = answers[c] * near[c]
+                main = term if c == 0 else main + term if c < 3 else main - term
+            return [main, answers[6] * near[2] - answers[7] * near[5], -(answers[7] * near[2]) - answers[6] * near[5]]
+
+        def sweep2(z, tile):
+            out = finish(z, a1, x1, 8)
+            for c in range(8):
+                a2[plane(c * D + z), :] = out[c]
+            outside = unpack(xf[0], z, 4) + unpack(xf[1], z, 2)
+            near = [f[plane(c * D + z), :] - outside[c] for c in range(6)]
+            share = [jnp.where(outer_x, v, 0.0) for v in shares(out, near)]
+            for k in range(3):
+                t[plane(k * D + z), :] = share[k]
+            return pack(z, (tile,), share)[0]
+
+        xs2[0] = each(D, sweep2, zero, WIDTH['sweep2'])
+        hz2 = []
+        hy2 = []
+        for side, z in ((0, 0), (1, D - 1)):
+            at = [pl.ds((c * D + z) * H, H) for c in range(8)]
+            near = [f[at[c], :] - zrf[side, pl.ds(c * H, H), :] for c in range(6)]
+            share = shares([a2[where, :] for where in at], near)
+            for k in range(3):
+                zs2[side, pl.ds(k * H, H), :] = share[k]
+            hz2.append(share)
+            at = [pl.ds(c * D * H + side * (H - 1), D, stride=H) for c in range(8)]
+            near = [f[at[c], :] - yrf[side, pl.ds(c * D, D), :] for c in range(6)]
+            share = shares([a2[where, :] for where in at], near)
+            for k in range(3):
+                ys2[side, pl.ds(k * D, D), :] = share[k]
+            hy2.append(share)
+        got2 = exchange(18, zs2, zr2, ys2, yr2, xs2, xr2)
+
+        def sens(z, last):
+            zp = clamp(z + 1)
+            av = [a2[plane(c * D + z), :] for c in range(8)]
+            fv = [f[plane(c * D + z), :] for c in range(6)]
+            above = [a2[plane(c * D + zp), :] for c in range(8)], [f[plane(c * D + zp), :] for c in range(6)]
+            ez = shares([v - w for v, w in zip(av, above[0])], [v - w for v, w in zip(fv, above[1])])
+            ey = shares([v - pltpu.roll(v, H - 1, 0) for v in av], [v - pltpu.roll(v, H - 1, 0) for v in fv])
+            ex = shares([v - pltpu.roll(v, L - 1, 1) for v in av], [v - pltpu.roll(v, L - 1, 1) for v in fv])
+            more = [zero, av[6] * fv[5] + av[7] * fv[2], av[6] * fv[2] - av[7] * fv[5]]
+            for c in range(6):
+                more[0] = more[0] + fv[c] * (fv[c] + av[(c + 3) % 6])
+            for k in range(3):
+                along_y = jnp.where(row < H - 1, ey[k], 0.0)
+                along_x = jnp.where(lane < L - 1, ex[k], 0.0)
+                energy = ez[k] + last[k] + along_y + pltpu.roll(along_y, 1, 0)
+                energy = energy + along_x + pltpu.roll(along_x, 1, 1) + t[plane(k * D + z), :]
+                s[plane(k * D + z), :] = kk[plane(z), :] * energy + qq[plane(z), :] * more[k]
+            return ez
+
+        each(D, sens, [zero] * 3, WIDTH['sens'])
+        total_ports = sum_finish("gz")
+        link_re = scale * jnp.sum(total_ports[0:1])
+        link_im = scale * jnp.sum(total_ports[1:2])
         imp_o[0] = link_re
         imp_o[1] = link_im
         coef_re = 2.0 * (link_re - zt[0])
         coef_im = -2.0 * (link_im - zt[1])
-        add_outer(zr1, yr1, 8)
-        x1 = [pair(xr1, 0), pair(xr1, 1)]
-
-        def sweep2(z, tile):
-            out = finish(z, a1, x1, 8)
-            out[2] = out[2] + (coef_re * out[6] - coef_im * out[7])
-            out[5] = out[5] + (coef_re * out[7] + coef_im * out[6])
-            for c in range(6):
-                a2[plane(c * D + z), :] = out[c]
-            outside = unpack(xf[0], z, 4) + unpack(xf[1], z, 2)
-            share = zero
-            for c in range(6):
-                term = out[c] * (f[plane(c * D + z), :] - outside[c])
-                share = share + term if c < 3 else share - term
-            share = jnp.where(outer_x, share, 0.0)
-            t[plane(z), :] = share
-            return pack(z, (tile,), [share])[0]
-
-        xs2[...] = lax.fori_loop(0, D, sweep2, zero)
-        adj_copy = pltpu.make_async_copy(a2, adj_o, out_sem)
-        adj_copy.start()
-        hz2 = []
-        hy2 = []
-        for side, z in ((0, 0), (1, D - 1)):
-            share = zero
-            for c in range(6):
-                here_ = pl.ds((c * D + z) * H, H)
-                term = a2[here_, :] * (f[here_, :] - zrf[side, pl.ds(c * H, H), :])
-                share = share + term if c < 3 else share - term
-            zs2[side] = share
-            hz2.append(share)
-            share = zero
-            for c in range(6):
-                at = pl.ds(c * D * H + side * (H - 1), D, stride=H)
-                term = a2[at, :] * (f[at, :] - yrf[side, pl.ds(c * D, D), :])
-                share = share + term if c < 3 else share - term
-            ys2[side] = share
-            hy2.append(share)
-        got2 = exchange(18, zs2, zr2, ys2, yr2, xs2, xr2)
-
-        def sens(z, last):
-            zp = jnp.minimum(z + 1, D - 1)
-            ez = zero
-            ey = zero
-            ex = zero
-            more = zero
-            av = [a2[plane(c * D + z), :] for c in range(6)]
-            fv = [f[plane(c * D + z), :] for c in range(6)]
-            for c in range(6):
-                a, g = av[c], fv[c]
-                tz = (a - a2[plane(c * D + zp), :]) * (g - f[plane(c * D + zp), :])
-                ty = (a - pltpu.roll(a, H - 1, 0)) * (g - pltpu.roll(g, H - 1, 0))
-                tx = (a - pltpu.roll(a, L - 1, 1)) * (g - pltpu.roll(g, L - 1, 1))
-                ez = ez + tz if c < 3 else ez - tz
-                ey = ey + ty if c < 3 else ey - ty
-                ex = ex + tx if c < 3 else ex - tx
-                more = more + g * (g + av[(c + 3) % 6])
-            ey = jnp.where(row < H - 1, ey, 0.0)
-            ex = jnp.where(lane < L - 1, ex, 0.0)
-            energy = ez + last + ey + pltpu.roll(ey, 1, 0) + ex + pltpu.roll(ex, 1, 1) + t[plane(z), :]
-            s[plane(z), :] = kk[plane(z), :] * energy + qq[plane(z), :] * more
-            return ez
-
-        lax.fori_loop(0, D, sens, zero)
+
+        def joined(parts):
+            return parts[0] + (coef_re * parts[1] + coef_im * parts[2])
+
+        def join(z, _):
+            s[plane(z), :] = joined([s[plane(k * D + z), :] for k in range(3)])
+            return 0
+
+        each(D, join, 0, WIDTH['join'])
+        for side, z in ((0, 0), (1, D - 1)):
+            at = pl.ds(z * H, H)
+            s[at, :] += kk[at, :] * joined(hz2[side])
+            at = pl.ds(side * (H - 1), D, stride=H)
+            s[at, :] = s[at, :] + kk[at, :] * joined(hy2[side])
         arrive(got2)
         for side, z in ((0, 0), (1, D - 1)):
             at = pl.ds(z * H, H)
-            s[at, :] += kk[at, :] * (hz2[side] + zr2[side])
+            s[at, :] += kk[at, :] * joined([zr2[side, pl.ds(k * H, H), :] for k in range(3)])
             at = pl.ds(side * (H - 1), D, stride=H)
-            s[at, :] = s[at, :] + kk[at, :] * (hy2[side] + yr2[side])
-        below = pltpu.roll(xr2[0], 1, 1)
-        above = pltpu.roll(xr2[1], L - 1, 1)
-        x2 = jnp.where(lax.rem(lane, 2) == 0, above, below)
+            s[at, :] = s[at, :] + kk[at, :] * joined([yr2[side, pl.ds(k * D, D), :] for k in range(3)])
+        tile2 = pair(xr2, 0)
+        tile2 = joined([tile2, pltpu.roll(tile2, L - 2, 1), pltpu.roll(tile2, L - 4, 1)])
 
         def split(v):
             high = v.astype(BF16)
             return high, (v - high.astype(F32)).astype(BF16)
 
         def add_x(z, _):
-            outside = unpack(x2, z, 1)[0]
+            outside = unpack(tile2, z, 1)[0]
             v = s[plane(z), :] + kk[plane(z), :] * jnp.where(outer_x, outside, 0.0)
             high, low = split(v)
             vb[plane(z), pl.ds(0, L)] = high
             vb[plane(z), pl.ds(L, L)] = low
             return 0
 
-        lax.fori_loop(0, D, add_x, 0)
+        each(D, add_x, 0, WIDTH['add_x'])
 
         def band(matrix, dst_low, dst_own, dst_high):
             for n, dst in ((0, dst_low), (2, dst_high), (1, dst_own)):
@@ -531,6 +543,16 @@
         gotF = []
         for side, d in ((0, -1), (1, 1)):
             gotF.append(beside("gy", d, ysF.at[side], yrF.at[1 - side], 24 + side))
+
+        def answer(z, _):
+            re, im = a2[plane(6 * D + z), :], a2[plane(7 * D + z), :]
+            a2[plane(2 * D + z), :] += coef_re * re - coef_im * im
+            a2[plane(5 * D + z), :] += coef_re * im + coef_im * re
+            return 0
+
+        each(D, answer, 0, WIDTH['answer'])
+        adj_copy = pltpu.make_async_copy(a2.at[pl.ds(0, 6 * D * H), :], adj_o, out_sem)
+        adj_copy.start()
         arrive(gotF)
 
         def add_y(z, _):
@@ -540,7 +562,7 @@
             vb[plane(z), pl.ds(L, L)] = low
             return 0
 
-        lax.fori_loop(0, D, add_y, 0)
+        each(D, add_y, 0, WIDTH['add_y'])
 
         band(kz, zsF.at[0], pb, zsF.at[1])
         gotZ = []
@@ -553,10 +575,10 @@
                     v = src[plane(p + 8 * half), :]
                     out = []
                     for side in (0, 1):
-                        moved = pltpu.roll(v, lax.rem(p * REACH + side * REACH, L), 1)
+                        moved = pltpu.roll(v, mod(p * REACH + side * REACH, L), 1)
                         out.append(jnp.where(lane // REACH == p, moved, tiles[side]))
                     return tuple(out)
-                tiles = lax.fori_loop(0, 8, step, (zero, zero))
+                tiles = each(8, step, (zero, zero), WIDTH['step'])
                 for side in (0, 1):
                     st[side, n, half] = tiles[side]
 
@@ -581,22 +603,23 @@
             def add_z(p, _):
                 at = plane(p + 8 * half)
                 v = pb[at, :] + zrF[0, at, :] + zrF[1, at, :]
-                back = lax.rem(L - p * REACH, L)
-                low = pltpu.roll(cols[0][half], lax.rem(back + L - REACH, L), 1)
+                back = mod(L - p * REACH, L)
+                low = pltpu.roll(cols[0][half], mod(back + L - REACH, L), 1)
                 high = pltpu.roll(cols[1][half], back, 1)
                 for k, part_ in enumerate((v, jnp.where(lane < L // 2, high, low))):
                     big, small = split(part_)
                     xin[at, pl.ds(k * L, L)] = big
                     xin[plane(p + 8 * half + D), pl.ds(k * L, L)] = small
                 return 0
-            lax.fori_loop(0, 8, add_z, 0)
+            each(8, add_z, 0, WIDTH['add_z'])
         both = lax.dot_general(xin[...], bx[...], (((1,), (1,)), ((), ())), preferred_element_type=F32)
         grad_o[...] = both[:D * H] + both[D * H:]
 
         for cond, copy in sent:
             pl.when(cond)(copy.wait_send)
-        loop(1, flat, lambda d: ar1_copy(d).wait_send())
-        loop(1, nz, lambda d: ar2_copy(d).wait_send())
+        for stage in stages:
+            for d in range(1, stages[stage][0]):
+                sum_copy(stage, d, False).wait_send()
         adj_copy.wait()
 
     return kernel
@@ -616,19 +639,17 @@
 
     scratch = [
         vm(6 * rows, L), vm(6 * rows, L), field, pltpu.VMEM((rows, L), jnp.int32), pltpu.VMEM((rows, L), jnp.int32),
-        vm(8 * rows, L), vm(6 * rows, L), vm(8 * rows, L),
-    ] + [field] * 14 + halo(7, 2) + halo(6, 2) + halo(8, 2) + [
-        vm(2, H, L), vm(2, D, L), vm(H, L), vm(2, H, L), vm(2, D, L), vm(2, H, L),
+        vm(8 * rows, L), vm(8 * rows, L), vm(8 * rows, L),
+    ] + [field] * 13 + [vm(3 * rows, L)] + halo(7, 2) + halo(6, 2) + halo(8, 2) + [
+        vm(2, 3 * H, L), vm(2, 3 * D, L), vm(1, H, L), vm(2, 3 * H, L), vm(2, 3 * D, L), vm(2, 1, H, L),
         pltpu.VMEM((3 * rows, 2 * L), BF16), pltpu.VMEM((3 * rows, 2 * L), BF16), pltpu.VMEM((L, 2 * L), BF16),
         field, vm(2, rows, L), vm(2, rows, L), vm(2, rows, L), vm(2, rows, L),
         vm(2, 3, 2, H, L), vm(2, 3, 2, H, L),
         pltpu.VMEM((rows, 2 * L), BF16), pltpu.VMEM((2 * rows, 2 * L), BF16),
-        vm(ny * nx, H, L), vm(nz, H, L),
+    ] + [vm(n, 2, L) for n in (CORES, nx, ny, nz // CORES)] + [
         pltpu.SemaphoreType.DMA((5,)), pltpu.SemaphoreType.DMA,
         pltpu.SemaphoreType.DMA((34,)), pltpu.SemaphoreType.DMA((34,)),
-        pltpu.SemaphoreType.DMA((ny * nx,)), pltpu.SemaphoreType.DMA((ny * nx,)),
-        pltpu.SemaphoreType.DMA((nz,)), pltpu.SemaphoreType.DMA((nz,)),
-    ]
+    ] + [pltpu.SemaphoreType.DMA((n,)) for n in (CORES, nx, ny, nz // CORES) for _ in range(2)]
     hbm = pl.BlockSpec(memory_space=pl.ANY)
     smem = pl.BlockSpec(memory_space=pltpu.SMEM)
     vmem = pl.BlockSpec(memory_space=pltpu.VMEM)
@@ -643,7 +664,7 @@
         out_specs=(hbm, vmem, smem),
         scratch_shapes=scratch,
         compiler_params=pltpu.CompilerParams(
-            collective_id=0, has_side_effects=True, vmem_limit_bytes=48 * 2**20),
+            collective_id=0, has_side_effects=True, vmem_limit_bytes=62 * 2**20),
     )
 
     def body(forward, adjoint_prev, density, labels, ports, z_target, radius_z, radius_y, radius_x):

time: 68.4 us -> 39.8 us (0.58)
  Pallas kernels: 59.7 us -> 35.6 us
  local copies, waits for them, and re-layouts: 7.71 us -> 3.31 us
    pallas_call x1, Pallas kernels: 59.7 us -> 35.6 us  [body(): call(forward.reshape(6 * rows, L), adjoint_prev.reshape(6 * rows, L), den...]
    unnamed x21 -> x7, local copies, waits for them, and re-layouts: 7.71 us -> 3.31 us
where the time goes in v2:
time: 39.8 us; the launch traced here: 39.6 us
  Pallas kernels  35.6 us (89%)
  local copies, waits for them, and re-layouts  3.31 us (8%)
  between operations  0.65 us (2%)
    pallas_call x1, Pallas kernels, body(): call(forward.reshape(6 * rows, L), adjoint_prev.reshape(6 * rows, L), den...  35.6 us
    unnamed x7, local copies, waits for them, and re-layouts  3.31 us

profile of v2, /device:TPU:1, one launch (start us, length us, event | category | flops | bytes accessed | tf_op | source)
XLA Modules:
  0.0 39.6 jit_solution(8725844095307898012)
XLA Ops:
  0.6 35.6 %shard_map.112 = (f32[1536,128]{1,0:T(8,128)}, f32[256,128]{1,0:T(8,128)}, f32[2]{0:T(128)}) custom-call(f32[1536,128]{1,0:T(8,128)} %bitcast.9, f32[1536,128]{1,0:T(8,128)} %bitcast.10, f32[256,128]{1,0:T(8,128)} %bitcast.12, s32[256,128]{1,0:T(8,128)} %bitcast.13, s32[256,128]{1,0:T(8,128)} %bitcast.14, f32[2]{0:T(128)} %zt.1, s32[256]{0:T(256)} %rz.1, ...), custom_call_target="tpu_custom_call" | custom-call | tf_op jit(solution)/shard_map/pallas_call | solution.py:671
  36.3 0.0 copy-start
  36.3 2.1 %copy.15 = f32[6,16,16,128]{3,2,1,0:T(8,128)} copy(f32[6,16,16,128]{3,2,1,0:T(8,128)} %bitcast.8) | data formatting | bytes 1572864
  38.4 0.0 copy-done
  38.4 0.0 copy-start.1
  38.4 0.7 %copy.16 = f32[16,16,128]{2,1,0:T(8,128)} copy(f32[16,16,128]{2,1,0:T(8,128)S(1)} %bitcast.11) | data formatting | bytes 262144
  39.1 0.0 copy-done.1
  39.1 0.5 %copy.17 = f32[2]{0:T(128)} copy(f32[2]{0:T(128)S(1)} %copy-done.1) | data formatting | bytes 16
Async XLA Ops:
  36.3 2.1 %copy-start = (f32[256,128]{1,0:T(8,128)S(1)}, f32[256,128]{1,0:T(8,128)}, u32[]{:S(2)}) copy-start(f32[256,128]{1,0:T(8,128)} %get-tuple-element.7) | copy-start | bytes 393220
  38.4 0.7 %copy-start.1 = (f32[2]{0:T(128)S(1)}, f32[2]{0:T(128)}, u32[]{:S(2)}) copy-start(f32[2]{0:T(128)} %get-tuple-element.14) | copy-start | bytes 28

commit v3 on v2

--- a/solution.py
+++ b/solution.py
@@ -11,7 +11,7 @@
 SENS_GAIN = 0.1
 REACH = 16
 CORES = 2
-WIDTH = dict(add_x=16, add_y=16, add_z=8, build=4, build_x=4, diagonal=16, faces=16, inner1=16, inner2=16, material=16, pack0=16, packf=16, sens=16, step=8, sweep1=16, sweep2=16, join=16, answer=16)
+WIDTH = dict(add_x=16, add_y=16, add_z=8, build=4, build_x=4, diagonal=16, faces=16, inner1=16, inner2=16, material=16, pack0=16, packf=16, sens=16, step=8, sweep1=16, sweep2=16, reluctivity=16, join=16, answer=16)
 MESH = pl.DeviceIdType.MESH
 AXES = ("gz", "gy", "gx")
 F32 = jnp.float32
@@ -66,16 +66,17 @@
     total = {"gz": nz * D, "gy": ny * H, "gx": nx * L}
     scale = 4.0 / (total["gz"] * total["gy"] * total["gx"])
 
-    def kernel(fwd_h, adj_h, den_h, lab_h, prt_h, zt, rz, ry, rx,
+    def kernel(fwd_h, adj_h, den_h, lab_h, prt_h, zt_h, rz_h, ry_h, rx_h,
                adj_o, grad_o, imp_o,
-               f, a0, den, lab, prt, a1, a2, t,
+               zt, rz, ry, rx, f, a0, den, lab, prt, a1, a2, t,
                nu, kap, wzm, wzp, wym, wyp, wxm, wxp, al, be, hx, kk, qq, s,
                zs0, ys0, xs0, zr0, yr0, xr0,
                zsf, ysf, xsf, zrf, yrf, xrf,
                zs1, ys1, xs1, zr1, yr1, xr1,
                zs2, ys2, xs2, zr2, yr2, xr2,
-               ky, kz, bx, pb, ysF, yrF, zsF, zrF, st, sr, vb, xin,
-               sum_core, sum_x, sum_y, sum_z, in_sem, out_sem, ss, rs,
+               ky, kz, bx, ysF, yrF, zsF, zrF, ysG, yrG, zsG, zrG, oyF, ozF, oyG, ozG,
+               stA, srA, stB, srB, vbA, vbB, xin,
+               sum_core, sum_x, sum_y, sum_z, in_sem, out_sem, grad, ss, rs,
                ss_core, rs_core, ss_x, rs_x, ss_y, rs_y, ss_z, rs_z):
         sums = {"core": sum_core, "gx": sum_x, "gy": sum_y, "gz": sum_z}
         sum_ss = {"core": ss_core, "gx": ss_x, "gy": ss_y, "gz": ss_z}
@@ -95,25 +96,33 @@
             "gz": (nz // CORES, lambda d: {"gz": lax.rem(gz + CORES * d, nz)}, gz // CORES),
         }
         barrier = pltpu.get_barrier_semaphore()
-        others = [(dz, dx, jnp.logical_and(inside("gz", dz), inside("gx", dx))) for dz in (-1, 1) for dx in (-1, 1)]
-        others += [(dz, 0, jnp.logical_and(inside("gz", dz), (core == 0) if dz < 0 else (core == CORES - 1)))
-                   for dz in (-1, 1)]
+        others = []
+        for axis, dx in (("gz", 1), ("gy", -1)):
+            for d in (-1, 1):
+                others.append(({axis: pos[axis] + d, "gx": gx + dx},
+                               jnp.logical_and(inside(axis, d), inside("gx", dx)),
+                               jnp.logical_and(inside(axis, -d), inside("gx", -dx))))
+        for d in (-1, 1):
+            near = jnp.logical_and(inside("gz", d), (core == 0) if d < 0 else (core == CORES - 1))
+            others.append(({"gz": gz + d}, near, near))
         expected = 0
         for members, peer, _ in stages.values():
             for d in range(1, members):
                 pl.semaphore_signal(barrier, inc=1, device_id=peer(d), device_id_type=MESH)
                 expected += 1
-        for dz, dx, cond in others:
-            @pl.when(cond)
+        for where, comes, goes in others:
+            @pl.when(comes)
             def _():
-                pl.semaphore_signal(barrier, inc=1, device_id={"gz": gz + dz, "gx": gx + dx}, device_id_type=MESH)
-            expected = expected + cond.astype(jnp.int32)
+                pl.semaphore_signal(barrier, inc=1, device_id=where, device_id_type=MESH)
+            expected = expected + goes.astype(jnp.int32)
 
         loads = [
             pltpu.make_async_copy(src, dst, in_sem.at[k])
-            for k, (src, dst) in enumerate(((den_h, den), (lab_h, lab), (adj_h, a0), (fwd_h, f), (prt_h, prt)))
+            for k, (src, dst) in enumerate((
+                (den_h, den), (lab_h, lab), (adj_h, a0), (fwd_h, f), (prt_h, prt),
+                (rx_h, rx), (ry_h, ry), (rz_h, rz), (zt_h, zt)))
         ]
-        for load in loads:
+        for load in loads[5:] + loads[:5]:
             load.start()
 
         def remote(src, dst, slot, where):
@@ -143,8 +152,8 @@
             return copies
 
         edges = {axis: (pos[axis] == 0, pos[axis] == {"gz": nz, "gy": ny, "gx": nx}[axis] - 1) for axis in AXES}
-        for axis, bufs in (("gz", (zr0, zrf, zr1, zr2, zrF)), ("gy", (yr0, yrf, yr1, yr2, yrF)),
-                           ("gx", (xr0, xrf, xr1, xr2, sr))):
+        for axis, bufs in (("gz", (zr0, zrf, zr1, zr2, zrF, zrG)), ("gy", (yr0, yrf, yr1, yr2, yrF, yrG)),
+                           ("gx", (xr0, xrf, xr1, xr2))):
             for side in (0, 1):
                 @pl.when(edges[axis][side])
                 def _():
@@ -156,75 +165,111 @@
                     else:
                         buf = zr0 if axis == "gz" else yr0
                         buf[side, pl.ds(6 * H, H), :] = jnp.ones((H, L), F32)
-        for side, dz_ in ((0, 1), (1, 1)):
-            for low in (0, 1):
-                @pl.when(edges["gz"][low])
+        for strip, axis, side in ((srA, "gz", 1), (srB, "gy", 0)):
+            for cond, slots in ((edges["gx"][side], (0, 1, 2)), (edges[axis][0], (1,)), (edges[axis][1], (2,))):
+                @pl.when(cond)
                 def _():
-                    sr[side, 1 + low] = jnp.zeros(sr.shape[2:], F32)
+                    for slot in slots:
+                        strip[slot] = jnp.zeros(strip.shape[1:], F32)
 
         lane = lax.broadcasted_iota(jnp.int32, (H, L), 1)
         row = lax.broadcasted_iota(jnp.int32, (H, L), 0)
 
-        lane2 = lax.broadcasted_iota(jnp.int32, (H, 2 * L), 1)
-        row2 = lax.broadcasted_iota(jnp.int32, (H, 2 * L), 0)
-        low4 = lax.rem(lane2, H)
-        high4 = lane2 // H
-        ry_l = jnp.zeros((H, 2 * L), jnp.int32)
-        rz_l = jnp.zeros((H, 2 * L), jnp.int32)
-        ry_r = jnp.zeros((H, L), jnp.int32)
-        for b in range(H):
-            ry_b = ry[gy * H + b]
-            rz_b = rz[gz * D + b]
-            ry_l = jnp.where(low4 == b, ry_b, ry_l)
-            rz_l = jnp.where(high4 == b, rz_b, rz_l)
-            ry_r = jnp.where(row == b, ry_b, ry_r)
-
-        def build(k, _):
-            shift = (k // D - 1) * D
-            p = lax.rem(k, D)
-            band_y = jnp.maximum(ry_l + 1 - jnp.abs(low4 - (row2 + shift)), 0)
-            ky[plane(k), :] = jnp.where(high4 == p, band_y, 0).astype(F32).astype(BF16)
-            band_z = jnp.maximum(rz_l + 1 - jnp.abs(high4 - (p + shift)), 0)
-            kz[plane(k), :] = jnp.where(low4 == row2, band_z, 0).astype(F32).astype(BF16)
-            return 0
-
-        each(3 * D, build, 0, WIDTH['build'])
-        rx_own = jnp.broadcast_to(rx[pl.ds(gx, 1), :], (H, L))
-        rx_low = jnp.broadcast_to(rx[pl.ds(jnp.maximum(gx - 1, 0), 1), :], (H, L))
-        rx_high = jnp.broadcast_to(rx[pl.ds(jnp.minimum(gx + 1, nx - 1), 1), :], (H, L))
-
-        def build_x(k, _):
-            target = row + k * H
-            own = jnp.maximum(rx_own + 1 - jnp.abs(lane - target), 0)
-            low = jnp.maximum(rx_low + 1 - jnp.abs(lane - L - target), 0)
-            high = jnp.maximum(rx_high + 1 - jnp.abs(lane + L - target), 0)
-            bx[plane(k), pl.ds(0, L)] = own.astype(F32).astype(BF16)
-            bx[plane(k), pl.ds(L, L)] = jnp.where(lane < L // 2, high, low).astype(F32).astype(BF16)
-            return 0
-
-        each(L // H, build_x, 0, WIDTH['build_x'])
-        norm_yx = (norm_of(ry_r, gy * H + row, total["gy"]) * norm_of(rx_own, gx * L + lane, total["gx"])).astype(F32)
-
         loads[0].wait()
         loads[1].wait()
 
-        def material(z, _):
+        def reluctivity(z, _):
             density = den[plane(z), :]
             design = jnp.where(lab[plane(z), :] == 2, 1.0, 0.0).astype(F32)
-            square = density * density
-            cube = square * density
+            cube = density * density * density
             nu_design = 1.0 / (1.0 + MU_GAIN * cube)
             nu[plane(z), :] = 1.0 - design + design * nu_design
             kap[plane(z), :] = design * KAPPA_GAIN * cube
-            gz_i = gz * D + z
-            norm_z = norm_of(rz[gz_i], gz_i, total["gz"]).astype(F32)
-            inverse = SENS_GAIN / (norm_yx * norm_z)
-            nu_slope = -3.0 * MU_GAIN * design * square * nu_design * nu_design
-            kk[plane(z), :] = -0.5 * nu_slope * inverse
-            qq[plane(z), :] = 3.0 * KAPPA_GAIN * design * square * inverse
-            return 0
-
-        each(D, material, 0, WIDTH['material'])
+            return 0
+
+        each(D, reluctivity, 0, WIDTH['reluctivity'])
+
+        def pack(z, tiles, values):
+            out = list(tiles)
+            for c, v in enumerate(values):
+                moved = pltpu.roll(v, (z * 8 + 2 * (c % 4) + 1) % L, 1)
+                out[c // 4] = jnp.where(lane // 2 == z * 4 + c % 4, moved, out[c // 4])
+            return tuple(out)
+
+        def pair(xr, n):
+            below = pltpu.roll(xr[0, n], 1, 1)
+            above = pltpu.roll(xr[1, n], L - 1, 1)
+            return jnp.where(lax.rem(lane, 2) == 0, above, below)
+
+        def unpack(tile, z, count, first=0):
+            return [pltpu.roll(tile, (-z * 8 - 2 * c - 1) % L, 1) for c in range(first, first + count)]
+
+        zero = jnp.zeros((H, L), F32)
+
+        def cell_rows(ref, count, first):
+            return ref[pl.ds(first, count * D, stride=H), :]
+
+        loads[2].wait()
+        for side, z in ((0, 0), (1, D - 1)):
+            for c in range(6):
+                zs0[side, pl.ds(c * H, H), :] = a0[pl.ds((c * D + z) * H, H), :]
+            zs0[side, pl.ds(6 * H, H), :] = nu[pl.ds(z * H, H), :]
+            ys0[side, pl.ds(0, 6 * D), :] = cell_rows(a0, 6, side * (H - 1))
+            ys0[side, pl.ds(6 * D, D), :] = cell_rows(nu, 1, side * (H - 1))
+
+        def pack0(z, tiles):
+            return pack(z, tiles, [a0[plane(c * D + z), :] for c in range(6)] + [nu[plane(z), :]])
+
+        tiles = each(D, pack0, (zero, zero), WIDTH['pack0'])
+        xs0[0] = tiles[0]
+        xs0[1] = tiles[1]
+
+        pl.semaphore_wait(barrier, expected)
+        got0 = exchange(0, zs0, zr0, ys0, yr0, xs0, xr0)
+
+        def sum_copy(stage, d, arriving):
+            members, peer, slot = stages[stage]
+            at = lax.rem(slot + d, members) if arriving else slot
+            ref = sums[stage].at[at]
+            return pltpu.make_async_remote_copy(
+                src_ref=ref, dst_ref=ref, send_sem=sum_ss[stage].at[d], recv_sem=sum_rs[stage].at[at],
+                device_id=peer(d), device_id_type=MESH)
+
+        def sum_start(stage, value):
+            members, _, slot = stages[stage]
+            sums[stage][slot] = value
+            for d in range(1, members):
+                sum_copy(stage, d, False).start()
+
+        def sum_finish(stage):
+            members = stages[stage][0]
+            for d in range(1, members):
+                sum_copy(stage, d, True).wait_recv()
+            value = sums[stage][0]
+            for q in range(1, members):
+                value = value + sums[stage][q]
+            return value
+
+        loads[3].wait()
+        loads[4].wait()
+        for side, z in ((0, 0), (1, D - 1)):
+            for c in range(6):
+                zsf[side, pl.ds(c * H, H), :] = f[pl.ds((c * D + z) * H, H), :]
+            ysf[side] = cell_rows(f, 6, side * (H - 1))
+
+        def packf(z, carry):
+            tiles, re, im = carry
+            values = [f[plane(c * D + z), :] for c in range(6)]
+            mask = prt[plane(z), :].astype(F32)
+            return (pack(z, tiles, values), re + mask * values[2], im + mask * values[5])
+
+        tiles, port_re, port_im = each(D, packf, ((zero, zero), zero, zero), WIDTH['packf'])
+        xsf[0] = tiles[0]
+        xsf[1] = tiles[1]
+        port_sum = jnp.concatenate(
+            [jnp.sum(port_re, axis=0, keepdims=True), jnp.sum(port_im, axis=0, keepdims=True)], axis=0)
+
+        sum_start("core", port_sum)
 
         def faces(z, _):
             v = nu[plane(z), :]
@@ -239,88 +284,6 @@
             return 0
 
         each(D, faces, 0, WIDTH['faces'])
-
-        def pack(z, tiles, values):
-            out = list(tiles)
-            for c, v in enumerate(values):
-                moved = pltpu.roll(v, (z * 8 + 2 * (c % 4) + 1) % L, 1)
-                out[c // 4] = jnp.where(lane // 2 == z * 4 + c % 4, moved, out[c // 4])
-            return tuple(out)
-
-        def pair(xr, n):
-            below = pltpu.roll(xr[0, n], 1, 1)
-            above = pltpu.roll(xr[1, n], L - 1, 1)
-            return jnp.where(lax.rem(lane, 2) == 0, above, below)
-
-        def unpack(tile, z, count, first=0):
-            return [pltpu.roll(tile, (-z * 8 - 2 * c - 1) % L, 1) for c in range(first, first + count)]
-
-        zero = jnp.zeros((H, L), F32)
-
-        def cell_rows(ref, count, first):
-            return ref[pl.ds(first, count * D, stride=H), :]
-
-        loads[2].wait()
-        for side, z in ((0, 0), (1, D - 1)):
-            for c in range(6):
-                zs0[side, pl.ds(c * H, H), :] = a0[pl.ds((c * D + z) * H, H), :]
-            zs0[side, pl.ds(6 * H, H), :] = nu[pl.ds(z * H, H), :]
-            ys0[side, pl.ds(0, 6 * D), :] = cell_rows(a0, 6, side * (H - 1))
-            ys0[side, pl.ds(6 * D, D), :] = cell_rows(nu, 1, side * (H - 1))
-
-        def pack0(z, tiles):
-            return pack(z, tiles, [a0[plane(c * D + z), :] for c in range(6)] + [nu[plane(z), :]])
-
-        tiles = each(D, pack0, (zero, zero), WIDTH['pack0'])
-        xs0[0] = tiles[0]
-        xs0[1] = tiles[1]
-
-        loads[3].wait()
-        loads[4].wait()
-        for side, z in ((0, 0), (1, D - 1)):
-            for c in range(6):
-                zsf[side, pl.ds(c * H, H), :] = f[pl.ds((c * D + z) * H, H), :]
-            ysf[side] = cell_rows(f, 6, side * (H - 1))
-
-        def packf(z, carry):
-            tiles, re, im = carry
-            values = [f[plane(c * D + z), :] for c in range(6)]
-            mask = prt[plane(z), :].astype(F32)
-            return (pack(z, tiles, values), re + mask * values[2], im + mask * values[5])
-
-        tiles, port_re, port_im = each(D, packf, ((zero, zero), zero, zero), WIDTH['packf'])
-        xsf[0] = tiles[0]
-        xsf[1] = tiles[1]
-        port_sum = jnp.concatenate(
-            [jnp.sum(port_re, axis=0, keepdims=True), jnp.sum(port_im, axis=0, keepdims=True)], axis=0)
-
-        pl.semaphore_wait(barrier, expected)
-        got0 = exchange(0, zs0, zr0, ys0, yr0, xs0, xr0)
-
-        def sum_copy(stage, d, arriving):
-            members, peer, slot = stages[stage]
-            at = lax.rem(slot + d, members) if arriving else slot
-            ref = sums[stage].at[at]
-            return pltpu.make_async_remote_copy(
-                src_ref=ref, dst_ref=ref, send_sem=sum_ss[stage].at[d], recv_sem=sum_rs[stage].at[at],
-                device_id=peer(d), device_id_type=MESH)
-
-        def sum_start(stage, value):
-            members, _, slot = stages[stage]
-            sums[stage][slot] = value
-            for d in range(1, members):
-                sum_copy(stage, d, False).start()
-
-        def sum_finish(stage):
-            members = stages[stage][0]
-            for d in range(1, members):
-                sum_copy(stage, d, True).wait_recv()
-            value = sums[stage][0]
-            for q in range(1, members):
-                value = value + sums[stage][q]
-            return value
-
-        sum_start("core", port_sum)
 
         def inner(a, count, z, begin):
             zm = clamp(z - 1)
@@ -427,6 +390,60 @@
             return 0
 
         each(D, inner2, 0, WIDTH['inner2'])
+        for load in loads[5:]:
+            load.wait()
+        ry_l = jnp.zeros((H, L), jnp.int32)
+        rz_l = jnp.zeros((H, L), jnp.int32)
+        ry_r = jnp.zeros((H, L), jnp.int32)
+        for b in range(H):
+            ry_b = ry[gy * H + b]
+            rz_b = rz[gz * D + b]
+            ry_l = jnp.where(lax.rem(lane, H) == b, ry_b, ry_l)
+            rz_l = jnp.where(lane // 8 == b, rz_b, rz_l)
+            ry_r = jnp.where(row == b, ry_b, ry_r)
+
+        def build(k, _):
+            n = k // 8
+            q = mod(k, 8)
+            band_y = jnp.maximum(ry_l + 1 - jnp.abs(lax.rem(lane, H) - (row + (n - 1) * H)), 0)
+            ky[plane(k), :] = jnp.where(lane // H == q, band_y, 0).astype(F32).astype(BF16)
+            band_z = jnp.maximum(rz_l + 1 - jnp.abs(lane // 8 - (2 * q + row // 8 + (n - 1) * D)), 0)
+            kz[plane(k), :] = jnp.where(lax.rem(lane, 8) == lax.rem(row, 8), band_z, 0).astype(F32).astype(BF16)
+            return 0
+
+        each(24, build, 0, WIDTH['build'])
+        rx_own = jnp.broadcast_to(rx[pl.ds(gx, 1), :], (H, L))
+        rx_low = jnp.broadcast_to(rx[pl.ds(jnp.maximum(gx - 1, 0), 1), :], (H, L))
+        rx_high = jnp.broadcast_to(rx[pl.ds(jnp.minimum(gx + 1, nx - 1), 1), :], (H, L))
+
+        def build_x(k, _):
+            target = row + k * H
+            own = jnp.maximum(rx_own + 1 - jnp.abs(lane - target), 0)
+            low = jnp.maximum(rx_low + 1 - jnp.abs(lane - L - target), 0)
+            high = jnp.maximum(rx_high + 1 - jnp.abs(lane + L - target), 0)
+            bx[plane(k), pl.ds(0, L)] = own.astype(F32).astype(BF16)
+            bx[plane(k), pl.ds(L, L)] = jnp.where(lane < L // 2, high, low).astype(F32).astype(BF16)
+            return 0
+
+        each(L // H, build_x, 0, WIDTH['build_x'])
+        norm_yx = (norm_of(ry_r, gy * H + row, total["gy"]) * norm_of(rx_own, gx * L + lane, total["gx"])).astype(F32)
+
+        def material(z, _):
+            density = den[plane(z), :]
+            design = jnp.where(lab[plane(z), :] == 2, 1.0, 0.0).astype(F32)
+            square = density * density
+            cube = square * density
+            nu_design = 1.0 / (1.0 + MU_GAIN * cube)
+            gz_i = gz * D + z
+            norm_z = norm_of(rz[gz_i], gz_i, total["gz"]).astype(F32)
+            inverse = SENS_GAIN / (norm_yx * norm_z)
+            nu_slope = -3.0 * MU_GAIN * design * square * nu_design * nu_design
+            kk[plane(z), :] = -0.5 * nu_slope * inverse
+            qq[plane(z), :] = 3.0 * KAPPA_GAIN * design * square * inverse
+            return 0
+
+        each(D, material, 0, WIDTH['material'])
+
         sum_start("gz", sum_finish("gy"))
         arrive(gotf)
         xf = [pair(xrf, 0), pair(xrf, 1)]
@@ -520,100 +537,132 @@
         tile2 = pair(xr2, 0)
         tile2 = joined([tile2, pltpu.roll(tile2, L - 2, 1), pltpu.roll(tile2, L - 4, 1)])
 
+        def add_x(z, _):
+            outside = unpack(tile2, z, 1)[0]
+            s[plane(z), :] += kk[plane(z), :] * jnp.where(outer_x, outside, 0.0)
+            return 0
+
+        each(D, add_x, 0, WIDTH['add_x'])
+
+        lane8 = lax.broadcasted_iota(jnp.int32, (8, L), 1)
+        left = lane < L // 2
+        left8 = lane8 < L // 2
+
+        def turn(v):
+            return pltpu.roll(v, L // 2, 1)
+
         def split(v):
             high = v.astype(BF16)
             return high, (v - high.astype(F32)).astype(BF16)
 
-        def add_x(z, _):
-            outside = unpack(tile2, z, 1)[0]
-            v = s[plane(z), :] + kk[plane(z), :] * jnp.where(outer_x, outside, 0.0)
+        def keep(ref, k, v):
             high, low = split(v)
-            vb[plane(z), pl.ds(0, L)] = high
-            vb[plane(z), pl.ds(L, L)] = low
-            return 0
-
-        each(D, add_x, 0, WIDTH['add_x'])
-
-        def band(matrix, dst_low, dst_own, dst_high):
+            ref[pl.ds(k * H, H), pl.ds(0, L)] = high
+            ref[pl.ds(k * H, H), pl.ds(L, L)] = low
+
+        def stack(a, b):
+            return jnp.concatenate([a, b], axis=0)
+
+        def band(matrix, value, dst_low, dst_own, dst_high):
             for n, dst in ((0, dst_low), (2, dst_high), (1, dst_own)):
-                both = jnp.dot(matrix[pl.ds(n * D * H, D * H), :], vb[...], preferred_element_type=F32)
+                both = jnp.dot(matrix[pl.ds(n * L, L), :], value[...], preferred_element_type=F32)
                 dst[...] = both[:, :L] + both[:, L:]
 
-        band(ky, ysF.at[0], pb, ysF.at[1])
-        gotF = []
-        for side, d in ((0, -1), (1, 1)):
-            gotF.append(beside("gy", d, ysF.at[side], yrF.at[1 - side], 24 + side))
+        def both_ways(axis, src, dst, slot):
+            return [beside(axis, d, src.at[side], dst.at[1 - side], slot + side) for side, d in ((0, -1), (1, 1))]
+
+        for p in range(8):
+            keep(vbA, p, jnp.where(left, s[plane(p), :], turn(s[plane(p + 8), :])))
+        band(ky, vbA, ysF.at[0], oyF, ysF.at[1])
+        gotY = both_ways("gy", ysF, yrF, 24)
+        for k in range(8):
+            tiles = []
+            for z in (2 * k, 2 * k + 1):
+                v = s[plane(z), :]
+                tiles.append(jnp.where(left8, turn(v[:8]), v[8:]))
+            keep(vbB, k, stack(*tiles))
+        band(kz, vbB, zsF.at[0], ozF, zsF.at[1])
+        gotZ = both_ways("gz", zsF, zrF, 26)
 
         def answer(z, _):
             re, im = a2[plane(6 * D + z), :], a2[plane(7 * D + z), :]
-            a2[plane(2 * D + z), :] += coef_re * re - coef_im * im
-            a2[plane(5 * D + z), :] += coef_re * im + coef_im * re
+            added = {2: coef_re * re - coef_im * im, 5: coef_re * im + coef_im * re}
+            for c in added:
+                a2[plane(c * D + z), :] += added[c]
             return 0
 
         each(D, answer, 0, WIDTH['answer'])
-        adj_copy = pltpu.make_async_copy(a2.at[pl.ds(0, 6 * D * H), :], adj_o, out_sem)
+        adj_copy = pltpu.make_async_copy(a2.at[pl.ds(0, 6 * D * H), :], adj_o, out_sem.at[0])
         adj_copy.start()
-        arrive(gotF)
-
-        def add_y(z, _):
-            v = pb[plane(z), :] + yrF[0, plane(z), :] + yrF[1, plane(z), :]
-            high, low = split(v)
-            vb[plane(z), pl.ds(0, L)] = high
-            vb[plane(z), pl.ds(L, L)] = low
-            return 0
-
-        each(D, add_y, 0, WIDTH['add_y'])
-
-        band(kz, zsF.at[0], pb, zsF.at[1])
-        gotZ = []
-        for side, d in ((0, -1), (1, 1)):
-            gotZ.append(beside("gz", d, zsF.at[side], zrF.at[1 - side], 26 + side))
-
-        def strips(src, n):
-            for half in range(2):
-                def step(p, tiles):
-                    v = src[plane(p + 8 * half), :]
-                    out = []
-                    for side in (0, 1):
-                        moved = pltpu.roll(v, mod(p * REACH + side * REACH, L), 1)
-                        out.append(jnp.where(lane // REACH == p, moved, tiles[side]))
-                    return tuple(out)
-                tiles = each(8, step, (zero, zero), WIDTH['step'])
-                for side in (0, 1):
-                    st[side, n, half] = tiles[side]
-
-        strips(zsF.at[0], 1)
-        strips(zsF.at[1], 2)
-        strips(pb, 0)
+
+        def eight(ref, k):
+            return ref[pl.ds(8 * k, 8), :]
+
+        arrive(gotZ)
+        vz = [eight(ozF, z) + eight(zrF.at[0], z) + eight(zrF.at[1], z) for z in range(D)]
+        for p in range(8):
+            low, high = vz[p], vz[p + 8]
+            keep(vbB, p, stack(jnp.where(left8, low, turn(high)), jnp.where(left8, turn(low), high)))
+        band(ky, vbB, ysG.at[0], oyG, ysG.at[1])
+        gotY2 = both_ways("gy", ysG, yrG, 30)
+        arrive(gotY)
+        vy = [oyF[plane(p), :] + yrF[0, plane(p), :] + yrF[1, plane(p), :] for p in range(8)]
+        for k in range(4):
+            near, far = [], []
+            for p in (2 * k, 2 * k + 1):
+                top, bottom = vy[p][:8], vy[p][8:]
+                near.append(jnp.where(left8, top, turn(bottom)))
+                far.append(jnp.where(left8, turn(top), bottom))
+            keep(vbA, k, stack(*near))
+            keep(vbA, k + 4, stack(*far))
+        band(kz, vbA, zsG.at[0], ozG, zsG.at[1])
+        gotZ2 = both_ways("gz", zsG, zrG, 28)
+
+        def columns(dst, src, count, rows_, offset, lanes):
+            for g in range(count // 4):
+                tile = None
+                for q in range(4):
+                    moved = pltpu.roll(src[pl.ds((4 * g + q) * rows_, rows_), :], (16 * q - offset) % L, 1)
+                    tile = moved if q == 0 else jnp.where(lax.rem(lanes // REACH, 4) == q, moved, tile)
+                dst[pl.ds(g * rows_, rows_), :] = tile
+
         gotX = []
-        for side, dx in ((0, -1), (1, 1)):
-            for n, dz in ((1, -1), (2, 1)):
-                go = jnp.logical_and(inside("gx", dx), inside("gz", dz))
-                come = jnp.logical_and(inside("gx", -dx), inside("gz", -dz))
-                copy = remote(st.at[side, n], sr.at[1 - side, 3 - n], 28 + side * 3 + n,
-                              {"gz": gz + dz, "gx": gx + dx})
+        for axis, dx, st, sr, src, slot in (("gy", 1, stB, srB, (oyG, ysG.at[0], ysG.at[1]), 35),
+                                            ("gz", -1, stA, srA, (ozG, zsG.at[0], zsG.at[1]), 32)):
+            for n, d in ((0, 0), (1, -1), (2, 1)):
+                if axis == "gz":
+                    columns(st.at[n], src[n], D, 8, 0, lane8)
+                else:
+                    columns(st.at[n], src[n], 8, H, 48, lane)
+                if d == 0:
+                    gotX.append(beside("gx", dx, st.at[0], sr.at[0], slot))
+                    continue
+                go = jnp.logical_and(inside("gx", dx), inside(axis, d))
+                come = jnp.logical_and(inside("gx", -dx), inside(axis, -d))
+                copy = remote(st.at[n], sr.at[3 - n], slot + n, {axis: pos[axis] + d, "gx": gx + dx})
                 pl.when(go)(copy.start)
                 sent.append((go, copy))
                 gotX.append((come, copy))
-            gotX.append(beside("gx", dx, st.at[side, 0], sr.at[1 - side, 0], 28 + side * 3))
-        arrive(gotZ)
+        arrive(gotY2)
+        arrive(gotZ2)
         arrive(gotX)
-        cols = [[sr[side, 0, half] + sr[side, 1, half] + sr[side, 2, half] for half in range(2)] for side in (0, 1)]
-        for half in range(2):
-            def add_z(p, _):
-                at = plane(p + 8 * half)
-                v = pb[at, :] + zrF[0, at, :] + zrF[1, at, :]
-                back = mod(L - p * REACH, L)
-                low = pltpu.roll(cols[0][half], mod(back + L - REACH, L), 1)
-                high = pltpu.roll(cols[1][half], back, 1)
-                for k, part_ in enumerate((v, jnp.where(lane < L // 2, high, low))):
-                    big, small = split(part_)
-                    xin[at, pl.ds(k * L, L)] = big
-                    xin[plane(p + 8 * half + D), pl.ds(k * L, L)] = small
-                return 0
-            each(8, add_z, 0, WIDTH['add_z'])
+        ga = [sum(srA[n, pl.ds(8 * g, 8), :] for n in range(3)) for g in range(4)]
+        gb = [sum(srB[n, plane(g), :] for n in range(3)) for g in range(2)]
+        vy = [oyG[plane(p), :] + yrG[0, plane(p), :] + yrG[1, plane(p), :] for p in range(8)]
+        for z in range(D):
+            v = eight(ozG, z) + eight(zrG.at[0], z) + eight(zrG.at[1], z)
+            own = jnp.where(left, stack(v, turn(v)), turn(vy[z]) if z < 8 else vy[z - 8])
+            group = ga[z // 4]
+            above = stack(*(pltpu.roll(group, (-16 * (z % 4) - 64 * h) % L, 1) for h in range(2)))
+            below = pltpu.roll(gb[z % 8 // 4], (112 - 64 * (z // 8) - 16 * (z % 4)) % L, 1)
+            for k, part in enumerate((own, jnp.where(left, above, below))):
+                big, small = split(part)
+                xin[plane(z), pl.ds(k * L, L)] = big
+                xin[plane(z + D), pl.ds(k * L, L)] = small
         both = lax.dot_general(xin[...], bx[...], (((1,), (1,)), ((), ())), preferred_element_type=F32)
-        grad_o[...] = both[:D * H] + both[D * H:]
+        grad[...] = both[:D * H] + both[D * H:]
+        grad_copy = pltpu.make_async_copy(grad, grad_o, out_sem.at[1])
+        grad_copy.start()
 
         for cond, copy in sent:
             pl.when(cond)(copy.wait_send)
@@ -621,6 +670,7 @@
             for d in range(1, stages[stage][0]):
                 sum_copy(stage, d, False).wait_send()
         adj_copy.wait()
+        grad_copy.wait()
 
     return kernel
 
@@ -638,21 +688,21 @@
         return [z, y, vm(tiles, H, L), z, y, vm(2, tiles, H, L)]
 
     scratch = [
+        pltpu.SMEM((2,), F32), pltpu.SMEM((nz * D,), jnp.int32), pltpu.SMEM((ny * H,), jnp.int32),
+        pltpu.VMEM((nx, L), jnp.int32),
         vm(6 * rows, L), vm(6 * rows, L), field, pltpu.VMEM((rows, L), jnp.int32), pltpu.VMEM((rows, L), jnp.int32),
         vm(8 * rows, L), vm(8 * rows, L), vm(8 * rows, L),
     ] + [field] * 13 + [vm(3 * rows, L)] + halo(7, 2) + halo(6, 2) + halo(8, 2) + [
         vm(2, 3 * H, L), vm(2, 3 * D, L), vm(1, H, L), vm(2, 3 * H, L), vm(2, 3 * D, L), vm(2, 1, H, L),
-        pltpu.VMEM((3 * rows, 2 * L), BF16), pltpu.VMEM((3 * rows, 2 * L), BF16), pltpu.VMEM((L, 2 * L), BF16),
-        field, vm(2, rows, L), vm(2, rows, L), vm(2, rows, L), vm(2, rows, L),
-        vm(2, 3, 2, H, L), vm(2, 3, 2, H, L),
-        pltpu.VMEM((rows, 2 * L), BF16), pltpu.VMEM((2 * rows, 2 * L), BF16),
+        pltpu.VMEM((3 * L, L), BF16), pltpu.VMEM((3 * L, L), BF16), pltpu.VMEM((L, 2 * L), BF16),
+    ] + [vm(2, L, L)] * 8 + [vm(L, L)] * 4 + [vm(3, 32, L)] * 4 + [
+        pltpu.VMEM((L, 2 * L), BF16), pltpu.VMEM((L, 2 * L), BF16), pltpu.VMEM((2 * rows, 2 * L), BF16),
     ] + [vm(n, 2, L) for n in (CORES, nx, ny, nz // CORES)] + [
-        pltpu.SemaphoreType.DMA((5,)), pltpu.SemaphoreType.DMA,
-        pltpu.SemaphoreType.DMA((34,)), pltpu.SemaphoreType.DMA((34,)),
+        pltpu.SemaphoreType.DMA((9,)), pltpu.SemaphoreType.DMA((2,)), field,
+        pltpu.SemaphoreType.DMA((38,)), pltpu.SemaphoreType.DMA((38,)),
     ] + [pltpu.SemaphoreType.DMA((n,)) for n in (CORES, nx, ny, nz // CORES) for _ in range(2)]
     hbm = pl.BlockSpec(memory_space=pl.ANY)
     smem = pl.BlockSpec(memory_space=pltpu.SMEM)
-    vmem = pl.BlockSpec(memory_space=pltpu.VMEM)
     call = pl.pallas_call(
         make_kernel(sizes),
         out_shape=(
@@ -660,18 +710,48 @@
             jax.ShapeDtypeStruct((rows, L), F32),
             jax.ShapeDtypeStruct((2,), F32),
         ),
-        in_specs=[hbm] * 5 + [smem] * 3 + [vmem],
-        out_specs=(hbm, vmem, smem),
+        in_specs=[hbm] * 9,
+        out_specs=(hbm, hbm, smem),
         scratch_shapes=scratch,
         compiler_params=pltpu.CompilerParams(
-            collective_id=0, has_side_effects=True, vmem_limit_bytes=62 * 2**20),
+            collective_id=0, has_side_effects=True, vmem_limit_bytes=60 * 2**20),
     )
 
+    parts = 4
+
+    def hand_over(adj_i, grad_i, imp_i, adj_o, grad_o, imp_o, adj, grad, imp, sem_in, sem_out):
+        size = 6 * rows // parts
+        pieces = [tuple(ref.at[pl.ds(k * size, size), :] for ref in (adj_i, adj, adj_o)) for k in range(parts)]
+        pieces += [(grad_i, grad, grad_o), (imp_i, imp, imp_o)]
+        loads = [pltpu.make_async_copy(src, mid, sem_in.at[k]) for k, (src, mid, _) in enumerate(pieces)]
+        stores = [pltpu.make_async_copy(mid, dst, sem_out.at[k]) for k, (_, mid, dst) in enumerate(pieces)]
+        for load in loads:
+            load.start()
+        for load, store in zip(loads, stores):
+            load.wait()
+            store.start()
+        for store in stores:
+            store.wait()
+
+    results = pl.pallas_call(
+        hand_over,
+        out_shape=(
+            jax.ShapeDtypeStruct((6 * rows, L), F32),
+            jax.ShapeDtypeStruct((rows, L), F32),
+            jax.ShapeDtypeStruct((2,), F32),
+        ),
+        in_specs=[hbm] * 3,
+        out_specs=(hbm,) * 3,
+        scratch_shapes=[
+            vm(6 * rows, L), vm(rows, L), pltpu.SMEM((2,), F32),
+            pltpu.SemaphoreType.DMA((parts + 2,)), pltpu.SemaphoreType.DMA((parts + 2,))],
+        compiler_params=pltpu.CompilerParams(vmem_limit_bytes=60 * 2**20))
+
     def body(forward, adjoint_prev, density, labels, ports, z_target, radius_z, radius_y, radius_x):
-        adjoint, gradient, impedance = call(
+        adjoint, gradient, impedance = results(*call(
             forward.reshape(6 * rows, L), adjoint_prev.reshape(6 * rows, L), density.reshape(rows, L),
             labels.reshape(rows, L), ports.reshape(rows, L), z_target, radius_z, radius_y,
-            radius_x.reshape(nx, L))
+            radius_x.reshape(nx, L)))
         return adjoint.reshape(6, D, H, L), gradient.reshape(D, H, L), impedance
 
     in_specs = (P(None, *AXES),) * 2 + (P(*AXES),) * 3 + (P(),) * 4

time: 39.8 us -> 36.8 us (0.925)
  local copies, waits for them, and re-layouts: 3.31 us -> 0 us
  Pallas kernels: 35.6 us -> 36 us
    unnamed x7 -> x0, local copies, waits for them, and re-layouts: 3.31 us -> none
    pallas_call x0 -> x1, Pallas kernels: none -> 2.05 us  [body(): results(*call(forward.reshape(6 * rows, L), adjoint_prev.reshape(6 * rows...]
    pallas_call x1, Pallas kernels: 35.6 us -> 33.9 us  [body(): call(forward.reshape(6 * rows, L), adjoint_prev.reshape(6 * rows, L), den...]
where the time goes in v3:
time: 36.8 us; the launch traced here: 36.6 us
  Pallas kernels  36 us (98%)
  between operations  0.64 us (2%)
    pallas_call x1, Pallas kernels, body(): call(forward.reshape(6 * rows, L), adjoint_prev.reshape(6 * rows, L), den...  33.9 us
    pallas_call x1, Pallas kernels, body(): results(*call(forward.reshape(6 * rows, L), adjoint_prev.reshape(6 * rows...  2.05 us

profile of v3, /device:TPU:1, one launch (start us, length us, event | category | flops | bytes accessed | tf_op | source)
XLA Modules:
  0.0 36.6 jit_solution(15040277514946368128)
XLA Ops:
  0.6 33.9 %shard_map.112 = (f32[1536,128]{1,0:T(8,128)}, f32[256,128]{1,0:T(8,128)}, f32[2]{0:T(128)}) custom-call(f32[1536,128]{1,0:T(8,128)} %bitcast.8, f32[1536,128]{1,0:T(8,128)} %bitcast.9, f32[256,128]{1,0:T(8,128)} %bitcast.10, s32[256,128]{1,0:T(8,128)} %bitcast.11, s32[256,128]{1,0:T(8,128)} %bitcast.12, f32[2]{0:T(128)} %zt_h.1, s32[256]{0:T(256)} %rz_h.1, ...), custom_call_target="tpu_custom_call" | custom-call | tf_op jit(solution)/shard_map/pallas_call | solution.py:751
  34.6 2.1 %shard_map.113 = (f32[1536,128]{1,0:T(8,128)}, f32[256,128]{1,0:T(8,128)}, f32[2]{0:T(128)}) custom-call(f32[1536,128]{1,0:T(8,128)} %get-tuple-element.9.adj_i, f32[256,128]{1,0:T(8,128)} %get-tuple-element.10.grad_i, f32[2]{0:T(128)} %get-tuple-element.11.imp_i), custom_call_target="tpu_custom_call" | custom-call | tf_op jit(solution)/shard_map/pallas_call | solution.py:751

commit v4 on v3

--- a/solution.py
+++ b/solution.py
@@ -11,7 +11,7 @@
 SENS_GAIN = 0.1
 REACH = 16
 CORES = 2
-WIDTH = dict(add_x=16, add_y=16, add_z=8, build=4, build_x=4, diagonal=16, faces=16, inner1=16, inner2=16, material=16, pack0=16, packf=16, sens=16, step=8, sweep1=16, sweep2=16, reluctivity=16, join=16, answer=16)
+WIDTH = dict(add_x=16, add_y=16, add_z=8, build=4, build_x=4, faces=16, inner1=16, inner2=16, material=16, pack0=16, packf=16, sens=16, step=8, sweep1=16, sweep2=16, reluctivity=16, join=16, answer=16)
 MESH = pl.DeviceIdType.MESH
 AXES = ("gz", "gy", "gx")
 F32 = jnp.float32
@@ -76,7 +76,7 @@
                zs2, ys2, xs2, zr2, yr2, xr2,
                ky, kz, bx, ysF, yrF, zsF, zrF, ysG, yrG, zsG, zrG, oyF, ozF, oyG, ozG,
                stA, srA, stB, srB, vbA, vbB, xin,
-               sum_core, sum_x, sum_y, sum_z, in_sem, out_sem, grad, ss, rs,
+               sum_core, sum_x, sum_y, sum_z, in_sem, out_sem, ss, rs,
                ss_core, rs_core, ss_x, rs_x, ss_y, rs_y, ss_z, rs_z):
         sums = {"core": sum_core, "gx": sum_x, "gy": sum_y, "gz": sum_z}
         sum_ss = {"core": ss_core, "gx": ss_x, "gy": ss_y, "gz": ss_z}
@@ -144,7 +144,7 @@
 
         def exchange(base, zs, zr, ys, yr, xs, xr):
             copies = []
-            for axis, src, dst, k in (("gy", ys, yr, 2), ("gx", xs, xr, 4), ("gz", zs, zr, 0)):
+            for axis, src, dst, k in (("gy", ys, yr, 2), ("gz", zs, zr, 0), ("gx", xs, xr, 4)):
                 for d in (-1, 1):
                     side = 0 if d < 0 else 1
                     piece = src if axis == "gx" else src.at[side]
@@ -281,6 +281,8 @@
             wyp[plane(z), :] = jnp.where(row < H - 1, 0.5 * (v + pltpu.roll(v, H - 1, 0)), 0.0)
             wxm[plane(z), :] = jnp.where(lane > 0, 0.5 * (v + pltpu.roll(v, 1, 1)), 0.0)
             wxp[plane(z), :] = jnp.where(lane < L - 1, 0.5 * (v + pltpu.roll(v, L - 1, 1)), 0.0)
+            inner_sum = wzm[plane(z), :] + wzp[plane(z), :] + wym[plane(z), :] + wyp[plane(z), :]
+            al[plane(z), :] = inner_sum + wxm[plane(z), :] + wxp[plane(z), :]
             return 0
 
         each(D, faces, 0, WIDTH['faces'])
@@ -325,16 +327,6 @@
                     t[at, :] = t[at, :] + hy[side] * yr[side, pl.ds(c * D, D), :]
 
         add_outer(zr0, yr0, 6)
-        def diagonal(z, _):
-            total_ = wzm[plane(z), :] + wzp[plane(z), :] + wym[plane(z), :] + wyp[plane(z), :]
-            v = nu[plane(z), :]
-            outside = unpack(x0[1], z, 1, 2)[0]
-            face = jnp.where(outer_x, 0.5 * (v + outside), 0.0)
-            hx[plane(z), :] = face
-            al[plane(z), :] = total_ + wxm[plane(z), :] + wxp[plane(z), :] + face
-            return 0
-
-        each(D, diagonal, 0, WIDTH['diagonal'])
         for side, z in ((0, 0), (1, D - 1)):
             al[pl.ds(z * H, H), :] += hz[side]
             at = pl.ds(side * (H - 1), D, stride=H)
@@ -354,7 +346,9 @@
             return out
 
         def sweep1(z, tiles):
-            d = al[plane(z), :]
+            face = jnp.where(outer_x, 0.5 * (nu[plane(z), :] + unpack(x0[1], z, 1, 2)[0]), 0.0)
+            hx[plane(z), :] = face
+            d = al[plane(z), :] + face
             kappa = kap[plane(z), :]
             weight = RELAX / (d * d + kappa * kappa)
             al[plane(z), :] = d * weight
@@ -592,7 +586,7 @@
             return 0
 
         each(D, answer, 0, WIDTH['answer'])
-        adj_copy = pltpu.make_async_copy(a2.at[pl.ds(0, 6 * D * H), :], adj_o, out_sem.at[0])
+        adj_copy = pltpu.make_async_copy(a2.at[pl.ds(0, 6 * D * H), :], adj_o, out_sem)
         adj_copy.start()
 
         def eight(ref, k):
@@ -605,6 +599,33 @@
             keep(vbB, p, stack(jnp.where(left8, low, turn(high)), jnp.where(left8, turn(low), high)))
         band(ky, vbB, ysG.at[0], oyG, ysG.at[1])
         gotY2 = both_ways("gy", ysG, yrG, 30)
+        def columns(dst, src, count, rows_, offset, lanes):
+            for g in range(count // 4):
+                tile = None
+                for q in range(4):
+                    moved = pltpu.roll(src[pl.ds((4 * g + q) * rows_, rows_), :], (16 * q - offset) % L, 1)
+                    tile = moved if q == 0 else jnp.where(lax.rem(lanes // REACH, 4) == q, moved, tile)
+                dst[pl.ds(g * rows_, rows_), :] = tile
+
+        def send_columns(axis, dx, st, sr, src, slot):
+            got = []
+            for n, d in ((0, 0), (1, -1), (2, 1)):
+                if axis == "gz":
+                    columns(st.at[n], src[n], D, 8, 0, lane8)
+                else:
+                    columns(st.at[n], src[n], 8, H, 48, lane)
+                if d == 0:
+                    got.append(beside("gx", dx, st.at[0], sr.at[0], slot))
+                    continue
+                go = jnp.logical_and(inside("gx", dx), inside(axis, d))
+                come = jnp.logical_and(inside("gx", -dx), inside(axis, -d))
+                copy = remote(st.at[n], sr.at[3 - n], slot + n, {axis: pos[axis] + d, "gx": gx + dx})
+                pl.when(go)(copy.start)
+                sent.append((go, copy))
+                got.append((come, copy))
+            return got
+
+        gotX = send_columns("gy", 1, stB, srB, (oyG, ysG.at[0], ysG.at[1]), 35)
         arrive(gotY)
         vy = [oyF[plane(p), :] + yrF[0, plane(p), :] + yrF[1, plane(p), :] for p in range(8)]
         for k in range(4):
@@ -618,31 +639,7 @@
         band(kz, vbA, zsG.at[0], ozG, zsG.at[1])
         gotZ2 = both_ways("gz", zsG, zrG, 28)
 
-        def columns(dst, src, count, rows_, offset, lanes):
-            for g in range(count // 4):
-                tile = None
-                for q in range(4):
-                    moved = pltpu.roll(src[pl.ds((4 * g + q) * rows_, rows_), :], (16 * q - offset) % L, 1)
-                    tile = moved if q == 0 else jnp.where(lax.rem(lanes // REACH, 4) == q, moved, tile)
-                dst[pl.ds(g * rows_, rows_), :] = tile
-
-        gotX = []
-        for axis, dx, st, sr, src, slot in (("gy", 1, stB, srB, (oyG, ysG.at[0], ysG.at[1]), 35),
-                                            ("gz", -1, stA, srA, (ozG, zsG.at[0], zsG.at[1]), 32)):
-            for n, d in ((0, 0), (1, -1), (2, 1)):
-                if axis == "gz":
-                    columns(st.at[n], src[n], D, 8, 0, lane8)
-                else:
-                    columns(st.at[n], src[n], 8, H, 48, lane)
-                if d == 0:
-                    gotX.append(beside("gx", dx, st.at[0], sr.at[0], slot))
-                    continue
-                go = jnp.logical_and(inside("gx", dx), inside(axis, d))
-                come = jnp.logical_and(inside("gx", -dx), inside(axis, -d))
-                copy = remote(st.at[n], sr.at[3 - n], slot + n, {axis: pos[axis] + d, "gx": gx + dx})
-                pl.when(go)(copy.start)
-                sent.append((go, copy))
-                gotX.append((come, copy))
+        gotX += send_columns("gz", -1, stA, srA, (ozG, zsG.at[0], zsG.at[1]), 32)
         arrive(gotY2)
         arrive(gotZ2)
         arrive(gotX)
@@ -660,9 +657,7 @@
                 xin[plane(z), pl.ds(k * L, L)] = big
                 xin[plane(z + D), pl.ds(k * L, L)] = small
         both = lax.dot_general(xin[...], bx[...], (((1,), (1,)), ((), ())), preferred_element_type=F32)
-        grad[...] = both[:D * H] + both[D * H:]
-        grad_copy = pltpu.make_async_copy(grad, grad_o, out_sem.at[1])
-        grad_copy.start()
+        grad_o[...] = both[:D * H] + both[D * H:]
 
         for cond, copy in sent:
             pl.when(cond)(copy.wait_send)
@@ -670,7 +665,6 @@
             for d in range(1, stages[stage][0]):
                 sum_copy(stage, d, False).wait_send()
         adj_copy.wait()
-        grad_copy.wait()
 
     return kernel
 
@@ -698,40 +692,39 @@
     ] + [vm(2, L, L)] * 8 + [vm(L, L)] * 4 + [vm(3, 32, L)] * 4 + [
         pltpu.VMEM((L, 2 * L), BF16), pltpu.VMEM((L, 2 * L), BF16), pltpu.VMEM((2 * rows, 2 * L), BF16),
     ] + [vm(n, 2, L) for n in (CORES, nx, ny, nz // CORES)] + [
-        pltpu.SemaphoreType.DMA((9,)), pltpu.SemaphoreType.DMA((2,)), field,
+        pltpu.SemaphoreType.DMA((9,)), pltpu.SemaphoreType.DMA,
         pltpu.SemaphoreType.DMA((38,)), pltpu.SemaphoreType.DMA((38,)),
     ] + [pltpu.SemaphoreType.DMA((n,)) for n in (CORES, nx, ny, nz // CORES) for _ in range(2)]
     hbm = pl.BlockSpec(memory_space=pl.ANY)
     smem = pl.BlockSpec(memory_space=pltpu.SMEM)
+    vmem = pl.BlockSpec(memory_space=pltpu.VMEM)
     call = pl.pallas_call(
         make_kernel(sizes),
         out_shape=(
-            jax.ShapeDtypeStruct((6 * rows, L), F32),
-            jax.ShapeDtypeStruct((rows, L), F32),
+            pltpu.VMEM((6 * rows, L), F32),
+            pltpu.VMEM((rows, L), F32),
             jax.ShapeDtypeStruct((2,), F32),
         ),
         in_specs=[hbm] * 9,
-        out_specs=(hbm, hbm, smem),
+        out_specs=(hbm, vmem, smem),
         scratch_shapes=scratch,
         compiler_params=pltpu.CompilerParams(
-            collective_id=0, has_side_effects=True, vmem_limit_bytes=60 * 2**20),
+            collective_id=0, has_side_effects=True, vmem_limit_bytes=32 * 2**20),
     )
 
-    parts = 4
-
-    def hand_over(adj_i, grad_i, imp_i, adj_o, grad_o, imp_o, adj, grad, imp, sem_in, sem_out):
-        size = 6 * rows // parts
-        pieces = [tuple(ref.at[pl.ds(k * size, size), :] for ref in (adj_i, adj, adj_o)) for k in range(parts)]
-        pieces += [(grad_i, grad, grad_o), (imp_i, imp, imp_o)]
-        loads = [pltpu.make_async_copy(src, mid, sem_in.at[k]) for k, (src, mid, _) in enumerate(pieces)]
-        stores = [pltpu.make_async_copy(mid, dst, sem_out.at[k]) for k, (_, mid, dst) in enumerate(pieces)]
-        for load in loads:
-            load.start()
-        for load, store in zip(loads, stores):
-            load.wait()
-            store.start()
-        for store in stores:
-            store.wait()
+    def hand_over(adj_i, grad_i, imp_i, adj_o, grad_o, imp_o, imp, sem, imp_sem):
+        first = pltpu.make_async_copy(imp_i, imp, imp_sem)
+        copies = [
+            pltpu.make_async_copy(src, dst, sem.at[k])
+            for k, (src, dst) in enumerate(((adj_i, adj_o), (grad_i, grad_o), (imp, imp_o)))
+        ]
+        first.start()
+        copies[0].start()
+        copies[1].start()
+        first.wait()
+        copies[2].start()
+        for copy in copies:
+            copy.wait()
 
     results = pl.pallas_call(
         hand_over,
@@ -742,16 +735,17 @@
         ),
         in_specs=[hbm] * 3,
         out_specs=(hbm,) * 3,
-        scratch_shapes=[
-            vm(6 * rows, L), vm(rows, L), pltpu.SMEM((2,), F32),
-            pltpu.SemaphoreType.DMA((parts + 2,)), pltpu.SemaphoreType.DMA((parts + 2,))],
-        compiler_params=pltpu.CompilerParams(vmem_limit_bytes=60 * 2**20))
+        scratch_shapes=[pltpu.SMEM((2,), F32), pltpu.SemaphoreType.DMA((3,)), pltpu.SemaphoreType.DMA],
+        compiler_params=pltpu.CompilerParams(vmem_limit_bytes=16 * 2**20))
 
     def body(forward, adjoint_prev, density, labels, ports, z_target, radius_z, radius_y, radius_x):
-        adjoint, gradient, impedance = results(*call(
+        arrays = (
             forward.reshape(6 * rows, L), adjoint_prev.reshape(6 * rows, L), density.reshape(rows, L),
             labels.reshape(rows, L), ports.reshape(rows, L), z_target, radius_z, radius_y,
-            radius_x.reshape(nx, L)))
+            radius_x.reshape(nx, L))
+        place = pltpu.with_memory_space_constraint
+        made = call(*(place(v, pltpu.HBM) for v in arrays))
+        adjoint, gradient, impedance = results(place(made[0], pltpu.VMEM), place(made[1], pltpu.VMEM), made[2])
         return adjoint.reshape(6, D, H, L), gradient.reshape(D, H, L), impedance
 
     in_specs = (P(None, *AXES),) * 2 + (P(*AXES),) * 3 + (P(),) * 4

time: 36.8 us -> 35.3 us (0.959)
  Pallas kernels: 36 us -> 34.6 us
    pallas_call x2, Pallas kernels: 36 us -> 34.6 us  [the longest x1 33.5 us: body(): made = call(*(place(v, pltpu.HBM) for v in arrays))]
where the time goes in v4:
time: 35.3 us; the launch traced here: 35.2 us
  Pallas kernels  34.6 us (98%)
  between operations  0.64 us (2%)
    pallas_call x1, Pallas kernels, body(): made = call(*(place(v, pltpu.HBM) for v in arrays))  33.5 us
    pallas_call x1, Pallas kernels, body(): results(place(made[0], pltpu.VMEM), place(made[1], pltpu.VMEM), made[2])  1.09 us

profile of v4, /device:TPU:1, one launch (start us, length us, event | category | flops | bytes accessed | tf_op | source)
XLA Modules:
  0.0 35.2 jit_solution(10450486083284822822)
XLA Ops:
  0.6 33.5 %shard_map.112 = (f32[1536,128]{1,0:T(8,128)S(1)}, f32[256,128]{1,0:T(8,128)S(1)}, f32[2]{0:T(128)S(1)}) custom-call(f32[1536,128]{1,0:T(8,128)} %bitcast.8, f32[1536,128]{1,0:T(8,128)} %bitcast.9, f32[256,128]{1,0:T(8,128)} %bitcast.10, s32[256,128]{1,0:T(8,128)} %bitcast.11, s32[256,128]{1,0:T(8,128)} %bitcast.12, f32[2]{0:T(128)} %zt_h.1, s32[256]{0:T(256)} %rz_h.1, ...), custom_call_target="tpu_custom_call" | custom-call | tf_op jit(solution)/shard_map/pallas_call | solution.py:747
  34.1 1.1 %shard_map.113 = (f32[1536,128]{1,0:T(8,128)}, f32[256,128]{1,0:T(8,128)}, f32[2]{0:T(128)}) custom-call(f32[1536,128]{1,0:T(8,128)S(1)} %get-tuple-element.9.adj_i, f32[256,128]{1,0:T(8,128)S(1)} %get-tuple-element.10.grad_i, f32[2]{0:T(128)S(1)} %get-tuple-element.11.imp_i), custom_call_target="tpu_custom_call" | custom-call | tf_op jit(solution)/shard_map/pallas_call | solution.py:748

commit v5 on v4

--- a/solution.py
+++ b/solution.py
@@ -11,7 +11,7 @@
 SENS_GAIN = 0.1
 REACH = 16
 CORES = 2
-WIDTH = dict(add_x=16, add_y=16, add_z=8, build=4, build_x=4, faces=16, inner1=16, inner2=16, material=16, pack0=16, packf=16, sens=16, step=8, sweep1=16, sweep2=16, reluctivity=16, join=16, answer=16)
+WIDTH = dict(add_x=16, add_y=16, add_z=8, build=4, build_x=4, faces=16, inner1=16, inner2=16, material=16, pack0=16, packf=16, sens=16, step=8, sweep1=16, sweep2=16, across_x=16, reluctivity=16, join=16, answer=16)
 MESH = pl.DeviceIdType.MESH
 AXES = ("gz", "gy", "gx")
 F32 = jnp.float32
@@ -68,7 +68,7 @@
 
     def kernel(fwd_h, adj_h, den_h, lab_h, prt_h, zt_h, rz_h, ry_h, rx_h,
                adj_o, grad_o, imp_o,
-               zt, rz, ry, rx, f, a0, den, lab, prt, a1, a2, t,
+               near_x, zt, rz, ry, rx, f, a0, den, lab, prt, a1, a2, t,
                nu, kap, wzm, wzp, wym, wyp, wxm, wxp, al, be, hx, kk, qq, s,
                zs0, ys0, xs0, zr0, yr0, xr0,
                zsf, ysf, xsf, zrf, yrf, xrf,
@@ -106,8 +106,8 @@
             near = jnp.logical_and(inside("gz", d), (core == 0) if d < 0 else (core == CORES - 1))
             others.append(({"gz": gz + d}, near, near))
         expected = 0
-        for members, peer, _ in stages.values():
-            for d in range(1, members):
+        for members, peer, _ in reversed(stages.values()):
+            for d in sorted(range(1, members), key=lambda d: abs(d - members / 2)):
                 pl.semaphore_signal(barrier, inc=1, device_id=peer(d), device_id_type=MESH)
                 expected += 1
         for where, comes, goes in others:
@@ -346,6 +346,8 @@
             return out
 
         def sweep1(z, tiles):
+            if z == 13:
+                sum_start("gy", sum_finish("gx"))
             face = jnp.where(outer_x, 0.5 * (nu[plane(z), :] + unpack(x0[1], z, 1, 2)[0]), 0.0)
             hx[plane(z), :] = face
             d = al[plane(z), :] + face
@@ -370,8 +372,6 @@
             ys1[side] = cell_rows(a1, 8, side * (H - 1))
         got1 = exchange(12, zs1, zr1, ys1, yr1, xs1, xr1)
 
-        sum_start("gy", sum_finish("gx"))
-
         def inner2(z, _):
             kappa = kap[plane(z), :]
 
@@ -441,6 +441,15 @@
         sum_start("gz", sum_finish("gy"))
         arrive(gotf)
         xf = [pair(xrf, 0), pair(xrf, 1)]
+
+        def across_x(z, _):
+            outside = unpack(xf[0], z, 4) + unpack(xf[1], z, 2)
+            for c in range(6):
+                at = plane(c * D + z)
+                near_x[at, :] = jnp.where(outer_x, f[at, :] - outside[c], 0.0)
+            return 0
+
+        each(D, across_x, 0, WIDTH['across_x'])
         arrive(got1)
         add_outer(zr1, yr1, 8)
         x1 = [pair(xr1, 0), pair(xr1, 1)]
@@ -456,9 +465,7 @@
             out = finish(z, a1, x1, 8)
             for c in range(8):
                 a2[plane(c * D + z), :] = out[c]
-            outside = unpack(xf[0], z, 4) + unpack(xf[1], z, 2)
-            near = [f[plane(c * D + z), :] - outside[c] for c in range(6)]
-            share = [jnp.where(outer_x, v, 0.0) for v in shares(out, near)]
+            share = shares(out, [near_x[plane(c * D + z), :] for c in range(6)])
             for k in range(3):
                 t[plane(k * D + z), :] = share[k]
             return pack(z, (tile,), share)[0]
@@ -557,26 +564,27 @@
         def stack(a, b):
             return jnp.concatenate([a, b], axis=0)
 
-        def band(matrix, value, dst_low, dst_own, dst_high):
-            for n, dst in ((0, dst_low), (2, dst_high), (1, dst_own)):
-                both = jnp.dot(matrix[pl.ds(n * L, L), :], value[...], preferred_element_type=F32)
-                dst[...] = both[:, :L] + both[:, L:]
-
-        def both_ways(axis, src, dst, slot):
-            return [beside(axis, d, src.at[side], dst.at[1 - side], slot + side) for side, d in ((0, -1), (1, 1))]
+        def band(matrix, value, n, dst):
+            both = jnp.dot(matrix[pl.ds(n * L, L), :], value[...], preferred_element_type=F32)
+            dst[...] = both[:, :L] + both[:, L:]
+
+        def band_out(matrix, value, axis, src, dst, own, slot):
+            band(matrix, value, 0, src.at[0])
+            band(matrix, value, 2, src.at[1])
+            got = [beside(axis, d, src.at[side], dst.at[1 - side], slot + side) for side, d in ((0, -1), (1, 1))]
+            band(matrix, value, 1, own)
+            return got
 
         for p in range(8):
             keep(vbA, p, jnp.where(left, s[plane(p), :], turn(s[plane(p + 8), :])))
-        band(ky, vbA, ysF.at[0], oyF, ysF.at[1])
-        gotY = both_ways("gy", ysF, yrF, 24)
+        gotY = band_out(ky, vbA, "gy", ysF, yrF, oyF, 24)
         for k in range(8):
             tiles = []
             for z in (2 * k, 2 * k + 1):
                 v = s[plane(z), :]
                 tiles.append(jnp.where(left8, turn(v[:8]), v[8:]))
             keep(vbB, k, stack(*tiles))
-        band(kz, vbB, zsF.at[0], ozF, zsF.at[1])
-        gotZ = both_ways("gz", zsF, zrF, 26)
+        gotZ = band_out(kz, vbB, "gz", zsF, zrF, ozF, 26)
 
         def answer(z, _):
             re, im = a2[plane(6 * D + z), :], a2[plane(7 * D + z), :]
@@ -597,8 +605,7 @@
         for p in range(8):
             low, high = vz[p], vz[p + 8]
             keep(vbB, p, stack(jnp.where(left8, low, turn(high)), jnp.where(left8, turn(low), high)))
-        band(ky, vbB, ysG.at[0], oyG, ysG.at[1])
-        gotY2 = both_ways("gy", ysG, yrG, 30)
+        gotY2 = band_out(ky, vbB, "gy", ysG, yrG, oyG, 30)
         def columns(dst, src, count, rows_, offset, lanes):
             for g in range(count // 4):
                 tile = None
@@ -636,18 +643,18 @@
                 far.append(jnp.where(left8, turn(top), bottom))
             keep(vbA, k, stack(*near))
             keep(vbA, k + 4, stack(*far))
-        band(kz, vbA, zsG.at[0], ozG, zsG.at[1])
-        gotZ2 = both_ways("gz", zsG, zrG, 28)
+        gotZ2 = band_out(kz, vbA, "gz", zsG, zrG, ozG, 28)
 
         gotX += send_columns("gz", -1, stA, srA, (ozG, zsG.at[0], zsG.at[1]), 32)
+        arrive(gotZ2)
+        vz = [eight(ozG, z) + eight(zrG.at[0], z) + eight(zrG.at[1], z) for z in range(D)]
         arrive(gotY2)
-        arrive(gotZ2)
         arrive(gotX)
         ga = [sum(srA[n, pl.ds(8 * g, 8), :] for n in range(3)) for g in range(4)]
         gb = [sum(srB[n, plane(g), :] for n in range(3)) for g in range(2)]
         vy = [oyG[plane(p), :] + yrG[0, plane(p), :] + yrG[1, plane(p), :] for p in range(8)]
         for z in range(D):
-            v = eight(ozG, z) + eight(zrG.at[0], z) + eight(zrG.at[1], z)
+            v = vz[z]
             own = jnp.where(left, stack(v, turn(v)), turn(vy[z]) if z < 8 else vy[z - 8])
             group = ga[z // 4]
             above = stack(*(pltpu.roll(group, (-16 * (z % 4) - 64 * h) % L, 1) for h in range(2)))
@@ -682,7 +689,7 @@
         return [z, y, vm(tiles, H, L), z, y, vm(2, tiles, H, L)]
 
     scratch = [
-        pltpu.SMEM((2,), F32), pltpu.SMEM((nz * D,), jnp.int32), pltpu.SMEM((ny * H,), jnp.int32),
+        vm(6 * rows, L), pltpu.SMEM((2,), F32), pltpu.SMEM((nz * D,), jnp.int32), pltpu.SMEM((ny * H,), jnp.int32),
         pltpu.VMEM((nx, L), jnp.int32),
         vm(6 * rows, L), vm(6 * rows, L), field, pltpu.VMEM((rows, L), jnp.int32), pltpu.VMEM((rows, L), jnp.int32),
         vm(8 * rows, L), vm(8 * rows, L), vm(8 * rows, L),

time: 35.3 us -> 34.5 us (0.977)
  Pallas kernels: 34.6 us -> 33.8 us
    pallas_call x1, Pallas kernels: 33.5 us -> 32.7 us  [body(): made = call(*(place(v, pltpu.HBM) for v in arrays))]
where the time goes in v5:
time: 34.5 us; the launch traced here: 34.4 us
  Pallas kernels  33.8 us (98%)
  between operations  0.64 us (2%)
    pallas_call x1, Pallas kernels, body(): made = call(*(place(v, pltpu.HBM) for v in arrays))  32.7 us
    pallas_call x1, Pallas kernels, body(): results(place(made[0], pltpu.VMEM), place(made[1], pltpu.VMEM), made[2])  1.09 us

profile of v5, /device:TPU:1, one launch (start us, length us, event | category | flops | bytes accessed | tf_op | source)
XLA Modules:
  0.0 34.4 jit_solution(5322181682807969707)
XLA Ops:
  0.6 32.7 %shard_map.112 = (f32[1536,128]{1,0:T(8,128)S(1)}, f32[256,128]{1,0:T(8,128)S(1)}, f32[2]{0:T(128)S(1)}) custom-call(f32[1536,128]{1,0:T(8,128)} %bitcast.8, f32[1536,128]{1,0:T(8,128)} %bitcast.9, f32[256,128]{1,0:T(8,128)} %bitcast.10, s32[256,128]{1,0:T(8,128)} %bitcast.11, s32[256,128]{1,0:T(8,128)} %bitcast.12, f32[2]{0:T(128)} %zt_h.1, s32[256]{0:T(256)} %rz_h.1, ...), custom_call_target="tpu_custom_call" | custom-call | tf_op jit(solution)/shard_map/pallas_call | solution.py:754
  33.3 1.1 %shard_map.113 = (f32[1536,128]{1,0:T(8,128)}, f32[256,128]{1,0:T(8,128)}, f32[2]{0:T(128)}) custom-call(f32[1536,128]{1,0:T(8,128)S(1)} %get-tuple-element.9.adj_i, f32[256,128]{1,0:T(8,128)S(1)} %get-tuple-element.10.grad_i, f32[2]{0:T(128)S(1)} %get-tuple-element.11.imp_i), custom_call_target="tpu_custom_call" | custom-call | tf_op jit(solution)/shard_map/pallas_call | solution.py:755

commit v6 on v5

--- a/solution.py
+++ b/solution.py
@@ -119,7 +119,8 @@
         loads = [
             pltpu.make_async_copy(src, dst, in_sem.at[k])
             for k, (src, dst) in enumerate((
-                (den_h, den), (lab_h, lab), (adj_h, a0), (fwd_h, f), (prt_h, prt),
+                (den_h, den), (lab_h, lab), (adj_h, a0.at[pl.ds(0, 6 * D * H), :]),
+                (fwd_h, f.at[pl.ds(0, 6 * D * H), :]), (prt_h, prt),
                 (rx_h, rx), (ry_h, ry), (rz_h, rz), (zt_h, zt)))
         ]
         for load in loads[5:] + loads[:5]:
@@ -691,9 +692,9 @@
     scratch = [
         vm(6 * rows, L), pltpu.SMEM((2,), F32), pltpu.SMEM((nz * D,), jnp.int32), pltpu.SMEM((ny * H,), jnp.int32),
         pltpu.VMEM((nx, L), jnp.int32),
-        vm(6 * rows, L), vm(6 * rows, L), field, pltpu.VMEM((rows, L), jnp.int32), pltpu.VMEM((rows, L), jnp.int32),
-        vm(8 * rows, L), vm(8 * rows, L), vm(8 * rows, L),
-    ] + [field] * 13 + [vm(3 * rows, L)] + halo(7, 2) + halo(6, 2) + halo(8, 2) + [
+        vm(6 * rows + H, L), vm(6 * rows + H, L), field, pltpu.VMEM((rows, L), jnp.int32), pltpu.VMEM((rows, L), jnp.int32),
+        vm(8 * rows + H, L), vm(8 * rows + H, L), vm(8 * rows + H, L),
+    ] + [vm(rows + H, L)] * 13 + [vm(3 * rows + H, L)] + halo(7, 2) + halo(6, 2) + halo(8, 2) + [
         vm(2, 3 * H, L), vm(2, 3 * D, L), vm(1, H, L), vm(2, 3 * H, L), vm(2, 3 * D, L), vm(2, 1, H, L),
         pltpu.VMEM((3 * L, L), BF16), pltpu.VMEM((3 * L, L), BF16), pltpu.VMEM((L, 2 * L), BF16),
     ] + [vm(2, L, L)] * 8 + [vm(L, L)] * 4 + [vm(3, 32, L)] * 4 + [

time: 34.5 us -> 34.5 us (level)
  no operation moved by 1% of the time
where the time goes in v6:
time: 34.5 us; the launch traced here: 34.4 us
  Pallas kernels  33.7 us (98%)
  between operations  0.64 us (2%)
    pallas_call x1, Pallas kernels, body(): made = call(*(place(v, pltpu.HBM) for v in arrays))  32.6 us
    pallas_call x1, Pallas kernels, body(): results(place(made[0], pltpu.VMEM), place(made[1], pltpu.VMEM), made[2])  1.09 us

profile of v6, /device:TPU:1, one launch (start us, length us, event | category | flops | bytes accessed | tf_op | source)
XLA Modules:
  0.0 34.4 jit_solution(2531954243050127288)
XLA Ops:
  0.6 32.6 %shard_map.112 = (f32[1536,128]{1,0:T(8,128)S(1)}, f32[256,128]{1,0:T(8,128)S(1)}, f32[2]{0:T(128)S(1)}) custom-call(f32[1536,128]{1,0:T(8,128)} %bitcast.8, f32[1536,128]{1,0:T(8,128)} %bitcast.9, f32[256,128]{1,0:T(8,128)} %bitcast.10, s32[256,128]{1,0:T(8,128)} %bitcast.11, s32[256,128]{1,0:T(8,128)} %bitcast.12, f32[2]{0:T(128)} %zt_h.1, s32[256]{0:T(256)} %rz_h.1, ...), custom_call_target="tpu_custom_call" | custom-call | tf_op jit(solution)/shard_map/pallas_call | solution.py:755
  33.3 1.1 %shard_map.113 = (f32[1536,128]{1,0:T(8,128)}, f32[256,128]{1,0:T(8,128)}, f32[2]{0:T(128)}) custom-call(f32[1536,128]{1,0:T(8,128)S(1)} %get-tuple-element.9.adj_i, f32[256,128]{1,0:T(8,128)S(1)} %get-tuple-element.10.grad_i, f32[2]{0:T(128)S(1)} %get-tuple-element.11.imp_i), custom_call_target="tpu_custom_call" | custom-call | tf_op jit(solution)/shard_map/pallas_call | solution.py:756

commit v7 on v6

--- a/solution.py
+++ b/solution.py
@@ -439,7 +439,6 @@
 
         each(D, material, 0, WIDTH['material'])
 
-        sum_start("gz", sum_finish("gy"))
         arrive(gotf)
         xf = [pair(xrf, 0), pair(xrf, 1)]
 
@@ -451,6 +450,7 @@
             return 0
 
         each(D, across_x, 0, WIDTH['across_x'])
+        sum_start("gz", sum_finish("gy"))
         arrive(got1)
         add_outer(zr1, yr1, 8)
         x1 = [pair(xr1, 0), pair(xr1, 1)]

time: 34.5 us -> 34.1 us (0.988)
    pallas_call x1, Pallas kernels: 32.6 us -> 32.3 us  [body(): made = call(*(place(v, pltpu.HBM) for v in arrays))]
where the time goes in v7:
time: 34.1 us; the launch traced here: 34 us
  Pallas kernels  33.4 us (98%)
  between operations  0.64 us (2%)
    pallas_call x1, Pallas kernels, body(): made = call(*(place(v, pltpu.HBM) for v in arrays))  32.3 us
    pallas_call x1, Pallas kernels, body(): results(place(made[0], pltpu.VMEM), place(made[1], pltpu.VMEM), made[2])  1.09 us

profile of v7, /device:TPU:1, one launch (start us, length us, event | category | flops | bytes accessed | tf_op | source)
XLA Modules:
  0.0 34.0 jit_solution(11278112640856163522)
XLA Ops:
  0.6 32.3 %shard_map.112 = (f32[1536,128]{1,0:T(8,128)S(1)}, f32[256,128]{1,0:T(8,128)S(1)}, f32[2]{0:T(128)S(1)}) custom-call(f32[1536,128]{1,0:T(8,128)} %bitcast.8, f32[1536,128]{1,0:T(8,128)} %bitcast.9, f32[256,128]{1,0:T(8,128)} %bitcast.10, s32[256,128]{1,0:T(8,128)} %bitcast.11, s32[256,128]{1,0:T(8,128)} %bitcast.12, f32[2]{0:T(128)} %zt_h.1, s32[256]{0:T(256)} %rz_h.1, ...), custom_call_target="tpu_custom_call" | custom-call | tf_op jit(solution)/shard_map/pallas_call | solution.py:755
  32.9 1.1 %shard_map.113 = (f32[1536,128]{1,0:T(8,128)}, f32[256,128]{1,0:T(8,128)}, f32[2]{0:T(128)}) custom-call(f32[1536,128]{1,0:T(8,128)S(1)} %get-tuple-element.9.adj_i, f32[256,128]{1,0:T(8,128)S(1)} %get-tuple-element.10.grad_i, f32[2]{0:T(128)S(1)} %get-tuple-element.11.imp_i), custom_call_target="tpu_custom_call" | custom-call | tf_op jit(solution)/shard_map/pallas_call | solution.py:756
